TPU v7x, 512 devices: a whole 4x8x8 slice. The times are simulated.
512 devices in a mesh: grp: 8 (over x, core), leaf: 64 (over y, z).
Axes of the slice: x: 4, y: 8, z: 8, core: 2. Of those that a mesh axis runs over, the one named last changes fastest.
Arguments:
- points: float32 [16, 1048576], P(None, ('grp', 'leaf')), may hold values from -6 to 6
- rhs: float32 [8, 1048576], P(None, ('grp', 'leaf')), may hold values from -6 to 6
- bases: float32 [8192, 64, 128], P(('grp', 'leaf')), may hold values from -0.5 to 0.5
- up_leaf: float32 [8192, 64, 64], P(('grp', 'leaf')), may hold values from -0.5 to 0.5
- up_cluster: float32 [512, 64, 64], P(('grp', 'leaf')), may hold values from -0.5 to 0.5
- coupling_leaf: float32 [8192, 4, 64, 64], P(('grp', 'leaf')), may hold values from -0.375 to 0.375
- coupling_cluster: float32 [512, 4, 64, 64], P(('grp', 'leaf')), may hold values from -0.09375 to 0.09375
- coupling_group: float32 [8, 8, 64, 64], P('grp'), may hold values from -0.03125 to 0.03125
- near_list: int32 [8192, 8], P(('grp', 'leaf')), may hold values from 0 to 8191, as said below
- near_count: int32 [8192], P(('grp', 'leaf')), may hold values from 1 to 8, as said below
- far_leaf: int32 [8192, 4], P(('grp', 'leaf')), may hold values from 0 to 8191, as said below
- far_cluster: int32 [512, 4], P(('grp', 'leaf')), may hold values from 0 to 511, as said below
Outputs:
- product: float32 [8, 1048576], P(None, ('grp', 'leaf'))
Inputs may be any that keep to these rules, and one draw needn't show every extreme that they name: `near_list`: slot 0 of row l is l itself; the other slots hold distinct leaves other than l, owned by the device of l or by the device just before or just after it, devices being ordered by grp then leaf, device d owning leaves d * 16 to d * 16 + 15. Only the first near_count[l] slots of row l of near_list are used. `far_leaf`: the entries of row l lie in the group of l, on distinct devices other than the device of l; taken over the 16 leaves of one device, at most 2 entries lie on any one device, and some device receives exactly that many. `far_cluster`: every entry of row c lies in the group of c, two or more places away from c within that group.
All inputs are finite; a program needn't handle non-finite values.
Results may differ from a plain program's by a relative error of at most 0.0003.
Values sent between devices are 32-bit elements; how exact they have to be, the bound alone decides.
A program may use at most 64 MiB of HBM per device.

v0:
```python
import jax
import jax.numpy as jnp
from jax import lax
from jax.sharding import PartitionSpec as P

HIGHEST = lax.Precision.HIGHEST
RATE = 0.8660254037844386


def padded(array, sides, width):
    edges = {}
    for axis, dim in sides:
        size, length = (lax.axis_size(axis), array.shape[dim])
        up = [(i, (i + 1) % size) for i in range(size - 1)]
        last = lax.slice_in_dim(array, length - width, length, axis=dim)
        first = lax.slice_in_dim(array, 0, width, axis=dim)
        edges[dim] = (
            lax.ppermute(last, axis, up),
            lax.ppermute(first, axis, [(b, a) for a, b in up]),
        )
    done = []
    for _, dim in sides:
        low, high = edges[dim]
        around = [(width, width) if d in done else (0, 0) for d in range(array.ndim)]
        array = jnp.concatenate([jnp.pad(low, around), array, jnp.pad(high, around)], axis=dim)
        done.append(dim)
    return array


def in_order(parts, dim):
    parts = jnp.moveaxis(parts, 0, dim)
    lengths = parts.shape
    return parts.reshape(*lengths[:dim], lengths[dim] * lengths[dim + 1], *lengths[dim + 2 :])


def one_gather(arrays, axis, dims):
    ravelled = jnp.concatenate([a.reshape(-1) for a in arrays])
    lines, at, done = (lax.all_gather(ravelled, axis), 0, [])
    for a, dim in zip(arrays, dims):
        parts = lines[:, at : at + a.size].reshape(-1, *a.shape)
        done.append(in_order(parts, dim))
        at += a.size
    return tuple(done)


def sent_to_all(array, axis):
    copies = jnp.broadcast_to(array, (lax.axis_size(axis), *array.shape))
    return lax.all_to_all(copies, axis, split_axis=0, concat_axis=0, tiled=True)


def gathered_copies(array, axis, dim):
    parts = sent_to_all(array, axis)
    return in_order(parts, dim)


def matern(left, right):
    cross = jnp.einsum("dbp,dbkq->bkpq", left, right, precision=HIGHEST)
    left_sq = jnp.sum(left * left, axis=0)
    right_sq = jnp.sum(right * right, axis=0)
    gap = left_sq[:, None, :, None] + right_sq[:, :, None, :] - 2.0 * cross
    scaled = RATE * jnp.sqrt(jnp.maximum(gap, 0.0))
    return (1.0 + scaled) * jnp.exp(-scaled)


def per_device(
    points,
    rhs,
    bases,
    up_leaf,
    up_cluster,
    coupling_leaf,
    coupling_cluster,
    coupling_group,
    near_list,
    near_count,
    far_leaf,
    far_cluster,
):
    dims = points.shape[0]
    nrhs = rhs.shape[0]
    leaf_dev, rank, leaf = bases.shape
    slots = near_list.shape[1]
    far_two = far_leaf.shape[1]
    n_leaf = lax.axis_size("leaf")
    n_grp = lax.axis_size("grp")
    grp_idx = lax.axis_index("grp")
    leaf_idx = lax.axis_index("leaf")
    device = grp_idx * n_leaf + leaf_idx
    stacked = jnp.concatenate([points, rhs], axis=0)
    extended = padded(stacked, ((("grp", "leaf"), 1),), points.shape[1])
    rhs_leaves = rhs.reshape(nrhs, leaf_dev, leaf)
    coef = jnp.einsum("lrp,slp->slr", bases, rhs_leaves, precision=HIGHEST)
    cluster_coef = jnp.einsum("slr,lrq->sq", coef, up_leaf, precision=HIGHEST)
    cluster_term = jnp.dot(cluster_coef, up_cluster[0], precision=HIGHEST)
    cluster_all, term_all = one_gather((cluster_coef, cluster_term), "leaf", (1, 1))
    group_sum = term_all.reshape(nrhs, n_leaf, rank).sum(axis=1)
    all_groups = gathered_copies(group_sum[None], "grp", 0)
    coords_local = points.reshape(dims, leaf_dev, leaf)
    ext_coords = extended[:dims].reshape(dims, 3 * leaf_dev, leaf)
    ext_values = extended[dims:].reshape(nrhs, 3 * leaf_dev, leaf)
    near_local = near_list - (device * leaf_dev - leaf_dev)
    block = 4
    nblocks = leaf_dev // block

    def one_block(item):
        left, index, count = item
        right = jnp.take(ext_coords, index.reshape(-1), axis=1).reshape(dims, block, slots, leaf)
        weights = jnp.take(ext_values, index.reshape(-1), axis=1).reshape(nrhs, block, slots, leaf)
        tile = matern(left, right)
        live = (jnp.arange(slots)[None, :] < count[:, None]).astype(jnp.float32)
        return jnp.einsum(
            "bkpq,sbkq->sbp", tile * live[:, :, None, None], weights, precision=HIGHEST
        )

    lefts = coords_local.reshape(dims, nblocks, block, leaf).transpose(1, 0, 2, 3)
    result = lax.map(
        one_block,
        (lefts, near_local.reshape(nblocks, block, slots), near_count.reshape(nblocks, block)),
    )
    near_out = result.transpose(1, 0, 2, 3).reshape(nrhs, leaf_dev * leaf)
    group_base = grp_idx * n_leaf
    leaf_base = group_base * leaf_dev
    many = leaf_dev * far_two
    span = n_leaf - 1
    capacity = (many + span - 1) // span
    asked_all = gathered_copies(far_leaf, "leaf", 0)
    asks = (asked_all - leaf_base).reshape(n_leaf, many)
    owners_all = asks // leaf_dev
    mine = owners_all == leaf_idx
    position = jnp.cumsum(mine.astype(jnp.int32), axis=1) - 1
    chosen = mine[:, :, None] & (
        position[:, :, None] == jnp.arange(capacity, dtype=jnp.int32)[None, None, :]
    )
    local_rows = jnp.sum(jnp.where(chosen, (asks % leaf_dev)[:, :, None], 0), axis=1)
    filled = jnp.any(chosen, axis=1).astype(jnp.float32)
    own_rows = coef.transpose(1, 0, 2).reshape(leaf_dev, nrhs * rank)
    outgoing = jnp.take(own_rows, local_rows.reshape(-1), axis=0).reshape(
        n_leaf, capacity, nrhs * rank
    )
    outgoing = outgoing * filled[:, :, None]
    incoming = lax.all_to_all(outgoing, "leaf", split_axis=0, concat_axis=0, tiled=True)
    own_asks = (far_leaf - leaf_base).reshape(many)
    own_owner = own_asks // leaf_dev
    hits = (own_owner[:, None] == jnp.arange(n_leaf, dtype=jnp.int32)[None, :]).astype(jnp.int32)
    own_pos = jnp.sum((jnp.cumsum(hits, axis=0) - 1) * hits, axis=1)
    flat_in = incoming.reshape(n_leaf * capacity, nrhs * rank)
    picked = jnp.take(flat_in, own_owner * capacity + own_pos, axis=0)
    picked = picked.reshape(leaf_dev, far_two, nrhs, rank)
    field = jnp.einsum("lkrq,lksq->slr", coupling_leaf, picked, precision=HIGHEST)
    cluster_pool = cluster_all.reshape(nrhs, n_leaf, rank)
    picked_cluster = jnp.take(cluster_pool, far_cluster[0] - group_base, axis=1)
    field_cluster = jnp.einsum(
        "krq,skq->sr", coupling_cluster[0], picked_cluster, precision=HIGHEST
    )
    others = (jnp.arange(n_grp) != grp_idx).astype(jnp.float32)
    field_group = jnp.einsum(
        "hrq,hsq->sr", coupling_group[0] * others[:, None, None], all_groups, precision=HIGHEST
    )
    field_cluster = field_cluster + jnp.einsum(
        "rq,sq->sr", up_cluster[0], field_group, precision=HIGHEST
    )
    field = field + jnp.einsum("lrq,sq->slr", up_leaf, field_cluster, precision=HIGHEST)
    far_out = jnp.einsum("lrp,slr->slp", bases, field, precision=HIGHEST).reshape(
        nrhs, leaf_dev * leaf
    )
    return far_out + near_out


def solution(mesh):
    placed = (
        P(None, ("grp", "leaf")),
        P(None, ("grp", "leaf")),
        P(("grp", "leaf"), None, None),
        P(("grp", "leaf"), None, None),
        P(("grp", "leaf"), None, None),
        P(("grp", "leaf"), None, None, None),
        P(("grp", "leaf"), None, None, None),
        P("grp", None, None, None),
        P(("grp", "leaf"), None),
        P(("grp", "leaf")),
        P(("grp", "leaf"), None),
        P(("grp", "leaf"), None),
    )
    return jax.shard_map(
        per_device, mesh=mesh, in_specs=placed, out_specs=P(None, ("grp", "leaf")), check_vma=False
    )
```

profile of v0, /device:TPU:1, one launch (start us, length us, event | category | flops | bytes accessed | tf_op | source)
XLA Modules:
  0.0 161.0 jit_solution(12447730678769685837)
XLA Ops:
  0.1 1.1 constant_dynamic-update-slice_fusion.1
  1.1 0.8 constant_dynamic-update-slice_fusion
  2.0 15.0 %collective-permute-start.1 = (f32[24,2048]{1,0:T(8,128)S(1)}, f32[24,2048]{1,0:T(8,128)S(1)}, u32[]{:S(2)}, u32[]{:S(2)}) collective-permute-start(f32[24,2048]{1,0:T(8,128)S(1)} %constant_dynamic-update-slice_fusion), channel_id=1, source_target_pairs={{1,0},{2,1},{3,2},{4,3},{5,4},{6,5},{7,6},{8,7},{9,8},{10,9},{11,1... | collective-permute-start | bytes 589832 | tf_op jit(solution)/shard_map/ppermute | solution.py:19
  16.9 1.9 %collective-permute-start = (f32[24,2048]{1,0:T(8,128)S(1)}, f32[24,2048]{1,0:T(8,128)}, u32[]{:S(2)}, u32[]{:S(2)}) collective-permute-start(f32[24,2048]{1,0:T(8,128)S(1)} %constant_dynamic-update-slice_fusion), channel_id=1, source_target_pairs={{0,1},{1,2},{2,3},{3,4},{4,5},{5,6},{6,7},{7,8},{8,9},{9,10},{10,1... | collective-permute-start | bytes 589832 | tf_op jit(solution)/shard_map/ppermute | solution.py:18
  18.9 2.0 %fusion.57 = f32[16,8,64]{2,1,0:T(8,128)S(1)} fusion(f32[16,64,128]{2,1,0:T(8,128)} %param.16, f32[8,2048]{1,0:T(8,128)} %param.15), kind=kOutput, calls=%fused_computation.83 | convolution fusion | flops 12582912 | bytes 622592 | tf_op jit(solution)/shard_map/lrp,slp->slr/dot_general | solution.py:92
  20.9 1.4 convolution_bitcast_fusion.4
  22.4 0.9 fusion.64
  23.4 37.2 %all-gather = f32[65536]{0:T(1024)S(1)} all-gather(f32[1024]{0:T(1024)S(1)} %pad_maximum_fusion.2), channel_id=2, replica_groups=mesh['grp'=8,'leaf'=64] {'leaf'}, dimensions={0}, use_global_device_ids=true | all-gather | bytes 266240 | tf_op jit(solution)/shard_map/all_gather | solution.py:38
  60.7 0.7 reshape.453
  61.4 16.4 %all-to-all-start.2 = ((f32[8,1,512]{2,1,0:T(1,128)}), f32[8,1,512]{2,1,0:T(1,128)S(1)}, u32[]{:S(2)}, u32[]{:S(2)}) async-start(f32[8,1,512]{2,1,0:T(1,128)} %reshape.453), calls=%async_computation.2 | async-start | bytes 32768 | tf_op jit(solution)/shard_map/all_to_all | solution.py:48
  79.9 2.5 %all-to-all-done.2 = f32[8,1,512]{2,1,0:T(1,128)S(1)} async-done(((f32[8,1,512]{2,1,0:T(1,128)}), f32[8,1,512]{2,1,0:T(1,128)S(1)}, u32[]{:S(2)}, u32[]{:S(2)}) %all-to-all-start.2) | async-done | bytes 16416 | tf_op jit(solution)/shard_map/all_to_all | solution.py:48
  83.1 7.5 %all-to-all-start = ((s32[64,16,4]{1,2,0:T(4,128)}), s32[64,16,4]{1,2,0:T(4,128)S(1)}, u32[]{:S(2)}, u32[]{:S(2)}) async-start(s32[64,16,4]{1,2,0:T(4,128)} %broadcast_in_dim.94), calls=%async_computation | async-start | bytes 262144 | tf_op jit(solution)/shard_map/all_to_all | solution.py:48
  91.2 0.7 reduce.3
  92.0 1.3 convolution_bitcast_fusion.2
  93.5 8.6 %all-to-all-done = s32[64,16,4]{1,2,0:T(4,128)S(1)} async-done(((s32[64,16,4]{1,2,0:T(4,128)}), s32[64,16,4]{1,2,0:T(4,128)S(1)}, u32[]{:S(2)}, u32[]{:S(2)}) %all-to-all-start) | async-done | bytes 16416 | tf_op jit(solution)/shard_map/all_to_all | solution.py:48
  103.1 0.8 gather_fusion.2
  104.2 0.9 select_multiply_fusion
  105.1 4.8 %all-to-all-start.1 = ((f32[64,2,512]{2,1,0:T(2,128)}), f32[64,2,512]{2,1,0:T(2,128)S(1)}, u32[]{:S(2)}, u32[]{:S(2)}) async-start(f32[64,2,512]{2,1,0:T(2,128)} %select_multiply_fusion), calls=%async_computation.1 | async-start | bytes 524288 | tf_op jit(solution)/shard_map/all_to_all | solution.py:141
  110.0 0.9 maximum_bitcast_fusion
  110.8 0.9 copy_bitcast_fusion
  111.8 43.8 %while.10 = (s32[]{:T(128)}, f32[4,8,4,128]{3,1,2,0:T(8,128)}, s32[4,4,8]{2,1,0:T(4,128)S(1)}, f32[8,48,128]{2,0,1:T(8,128)S(1)}, f32[4,16,4,128]{3,2,0,1:T(4,12...) while((s32[]{:T(128)}, f32[4,8,4,128]{3,1,2,0:T(8,128)}, ...), condition=%wide.region_9.10_spmd, body=%wide.region_6.9_spmd.sunk | while | flops 156021792 | bytes 5826621 | solution.py:116
  112.6 4.9 %fusion.110 = f32[4,8,128,128]{3,2,1,0:T(8,128)} fusion(f32[16,4,8,128]{3,0,2,1:T(8,128)S(1)} %bitcast.154, pred[4,8]{1,0:T(4,128)(4,1)S(1)} %get-tuple-element.155, f32[1,16,4,128]{3,2,0,1:T(4,128)S(1)} %constant_dynamic-slice_fusion.5), kind=kOutput, calls=%fused_computation.29.clone.1 | convolution fusion | flops 100728832 | bytes 2392096 | tf_op jit(solution)/shard_map/while/body/eval_jaxpr/dbp,dbkq->bkpq/dot_general | solution.py:57
  118.3 4.5 %fusion.113 = f32[4,8,4,128]{3,1,2,0:T(8,128)} fusion(f32[4,8,4,128]{3,1,2,0:T(8,128)} %get-tuple-element.166, s32[]{:T(128)S(6)} %copy.106, f32[4,8,128,128]{3,2,1,0:T(8,128)} %fusion.110, f32[4,8]{1,0:T(4,128)S(1)} %get-tuple-element.156, f32[4,8,128]{2,1,0:T(8,128)S(1)} %bitcast.157, f32[4,128]{1,0:T(4,128)S(1)} %fusion.112, ...), kind=kOutput, calls=%fused_computation.18.clone.1 | convolution fusion | flops 55083008 | bytes 2263204 | tf_op jit(solution)/shard_map/while/body/eval_jaxpr/bkpq,sbkq->sbp/dot_general | solution.py:111
  123.5 4.9 %fusion.110 = f32[4,8,128,128]{3,2,1,0:T(8,128)} fusion(f32[16,4,8,128]{3,0,2,1:T(8,128)S(1)} %bitcast.154, pred[4,8]{1,0:T(4,128)(4,1)S(1)} %get-tuple-element.155, f32[1,16,4,128]{3,2,0,1:T(4,128)S(1)} %constant_dynamic-slice_fusion.5), kind=kOutput, calls=%fused_computation.29.clone.1 | convolution fusion | flops 100728832 | bytes 2392096 | tf_op jit(solution)/shard_map/while/body/eval_jaxpr/dbp,dbkq->bkpq/dot_general | solution.py:57
  129.2 4.5 %fusion.113 = f32[4,8,4,128]{3,1,2,0:T(8,128)} fusion(f32[4,8,4,128]{3,1,2,0:T(8,128)} %get-tuple-element.166, s32[]{:T(128)S(6)} %copy.106, f32[4,8,128,128]{3,2,1,0:T(8,128)} %fusion.110, f32[4,8]{1,0:T(4,128)S(1)} %get-tuple-element.156, f32[4,8,128]{2,1,0:T(8,128)S(1)} %bitcast.157, f32[4,128]{1,0:T(4,128)S(1)} %fusion.112, ...), kind=kOutput, calls=%fused_computation.18.clone.1 | convolution fusion | flops 55083008 | bytes 2263204 | tf_op jit(solution)/shard_map/while/body/eval_jaxpr/bkpq,sbkq->sbp/dot_general | solution.py:111
  134.5 4.9 %fusion.110 = f32[4,8,128,128]{3,2,1,0:T(8,128)} fusion(f32[16,4,8,128]{3,0,2,1:T(8,128)S(1)} %bitcast.154, pred[4,8]{1,0:T(4,128)(4,1)S(1)} %get-tuple-element.155, f32[1,16,4,128]{3,2,0,1:T(4,128)S(1)} %constant_dynamic-slice_fusion.5), kind=kOutput, calls=%fused_computation.29.clone.1 | convolution fusion | flops 100728832 | bytes 2392096 | tf_op jit(solution)/shard_map/while/body/eval_jaxpr/dbp,dbkq->bkpq/dot_general | solution.py:57
  140.2 4.5 %fusion.113 = f32[4,8,4,128]{3,1,2,0:T(8,128)} fusion(f32[4,8,4,128]{3,1,2,0:T(8,128)} %get-tuple-element.166, s32[]{:T(128)S(6)} %copy.106, f32[4,8,128,128]{3,2,1,0:T(8,128)} %fusion.110, f32[4,8]{1,0:T(4,128)S(1)} %get-tuple-element.156, f32[4,8,128]{2,1,0:T(8,128)S(1)} %bitcast.157, f32[4,128]{1,0:T(4,128)S(1)} %fusion.112, ...), kind=kOutput, calls=%fused_computation.18.clone.1 | convolution fusion | flops 55083008 | bytes 2263204 | tf_op jit(solution)/shard_map/while/body/eval_jaxpr/bkpq,sbkq->sbp/dot_general | solution.py:111
  145.5 4.9 %fusion.110 = f32[4,8,128,128]{3,2,1,0:T(8,128)} fusion(f32[16,4,8,128]{3,0,2,1:T(8,128)S(1)} %bitcast.154, pred[4,8]{1,0:T(4,128)(4,1)S(1)} %get-tuple-element.155, f32[1,16,4,128]{3,2,0,1:T(4,128)S(1)} %constant_dynamic-slice_fusion.5), kind=kOutput, calls=%fused_computation.29.clone.1 | convolution fusion | flops 100728832 | bytes 2392096 | tf_op jit(solution)/shard_map/while/body/eval_jaxpr/dbp,dbkq->bkpq/dot_general | solution.py:57
  151.2 4.5 %fusion.113 = f32[4,8,4,128]{3,1,2,0:T(8,128)} fusion(f32[4,8,4,128]{3,1,2,0:T(8,128)} %get-tuple-element.166, s32[]{:T(128)S(6)} %copy.106, f32[4,8,128,128]{3,2,1,0:T(8,128)} %fusion.110, f32[4,8]{1,0:T(4,128)S(1)} %get-tuple-element.156, f32[4,8,128]{2,1,0:T(8,128)S(1)} %bitcast.157, f32[4,128]{1,0:T(4,128)S(1)} %fusion.112, ...), kind=kOutput, calls=%fused_computation.18.clone.1 | convolution fusion | flops 55083008 | bytes 2263204 | tf_op jit(solution)/shard_map/while/body/eval_jaxpr/bkpq,sbkq->sbp/dot_general | solution.py:111
  156.6 1.9 %convolution_bitcast_fusion.1 = f32[8,16,64]{2,0,1:T(8,128)S(1)} fusion(f32[16,4,64,64]{3,2,1,0:T(8,128)S(1)} %copy-done, f32[16,4,8,64]{3,2,1,0:T(8,128)S(1)} %gather.31, pred[16,4]{1,0:T(8,128)(4,1)S(1)} %compare_and_fusion.2), kind=kOutput, calls=%fused_computation.62 | convolution fusion | flops 25198592 | bytes 1212480 | tf_op jit(solution)/shard_map/lkrq,lksq->slr/dot_general | solution.py:149
  158.5 1.3 convolution_add_fusion
  159.8 1.2 fusion.46
  (130 shorter events, 12.6 us)
Async XLA Ops:
  0.0 156.6 %copy-start = (f32[16,4,64,64]{3,2,1,0:T(8,128)S(1)}, f32[16,4,64,64]{3,2,1,0:T(8,128)}, u32[]{:S(2)}) copy-start(f32[16,4,64,64]{3,2,1,0:T(8,128)} %param.19) | copy-start | bytes 3145732
  0.0 79.6 %copy-start.3 = (f32[16,2048]{1,0:T(8,128)S(1)}, f32[16,2048]{1,0:T(8,128)}, u32[]{:S(2)}) copy-start(f32[16,2048]{1,0:T(8,128)} %param.14) | copy-start | bytes 393220
  0.0 77.8 %copy-start.7 = (s32[16,4]{0,1:T(4,128)S(1)}, s32[16,4]{0,1:T(4,128)}, u32[]{:S(2)}) copy-start(s32[16,4]{0,1:T(4,128)} %param.24) | copy-start | bytes 772
  0.0 78.0 %copy-start.10 = (s32[1,4]{1,0:T(1,128)S(1)}, s32[1,4]{1,0:T(1,128)}, u32[]{:S(2)}) copy-start(s32[1,4]{1,0:T(1,128)} %param.25) | copy-start | bytes 52
  0.0 78.1 %copy-start.8 = (s32[16,8]{0,1:T(8,128)S(1)}, s32[16,8]{0,1:T(8,128)}, u32[]{:S(2)}) copy-start(s32[16,8]{0,1:T(8,128)} %param.22) | copy-start | bytes 1540
  0.0 79.3 %copy-start.4 = (f32[1,4,64,64]{3,2,1,0:T(8,128)S(1)}, f32[1,4,64,64]{3,2,1,0:T(8,128)}, u32[]{:S(2)}) copy-start(f32[1,4,64,64]{3,2,1,0:T(8,128)} %param.20) | copy-start | bytes 196612
  0.0 79.8 %copy-start.9 = (s32[16]{0:T(128)S(1)}, s32[16]{0:T(128)}, u32[]{:S(2)}) copy-start(s32[16]{0:T(128)} %param.23) | copy-start | bytes 196
  2.0 108.0 %collective-permute-start.1 = (f32[24,2048]{1,0:T(8,128)S(1)}, f32[24,2048]{1,0:T(8,128)S(1)}, u32[]{:S(2)}, u32[]{:S(2)}) collective-permute-start(f32[24,2048]{1,0:T(8,128)S(1)} %constant_dynamic-update-slice_fusion), channel_id=1, source_target_pairs={{1,0},{2,1},{3,2},{4,3},{5,4},{6,5},{7,6},{8,7},{9,8},{10,9},{11,1... | collective-permute-start | bytes 589832 | tf_op jit(solution)/shard_map/ppermute | solution.py:19
  16.9 93.0 %collective-permute-start = (f32[24,2048]{1,0:T(8,128)S(1)}, f32[24,2048]{1,0:T(8,128)}, u32[]{:S(2)}, u32[]{:S(2)}) collective-permute-start(f32[24,2048]{1,0:T(8,128)S(1)} %constant_dynamic-update-slice_fusion), channel_id=1, source_target_pairs={{0,1},{1,2},{2,3},{3,4},{4,5},{5,6},{6,7},{7,8},{8,9},{9,10},{10,1... | collective-permute-start | bytes 589832 | tf_op jit(solution)/shard_map/ppermute | solution.py:18
  20.9 72.4 %copy-start.5 = (f32[1,64,64]{2,1,0:T(8,128)S(1)}, f32[1,64,64]{2,1,0:T(8,128)}, u32[]{:S(2)}) copy-start(f32[1,64,64]{2,1,0:T(8,128)} %param.18) | copy-start | bytes 49156
  61.4 21.0 %all-to-all-start.2 = ((f32[8,1,512]{2,1,0:T(1,128)}), f32[8,1,512]{2,1,0:T(1,128)S(1)}, u32[]{:S(2)}, u32[]{:S(2)}) async-start(f32[8,1,512]{2,1,0:T(1,128)} %reshape.453), calls=%async_computation.2 | async-start | bytes 32768 | tf_op jit(solution)/shard_map/all_to_all | solution.py:48
  83.1 19.0 %all-to-all-start = ((s32[64,16,4]{1,2,0:T(4,128)}), s32[64,16,4]{1,2,0:T(4,128)S(1)}, u32[]{:S(2)}, u32[]{:S(2)}) async-start(s32[64,16,4]{1,2,0:T(4,128)} %broadcast_in_dim.94), calls=%async_computation | async-start | bytes 262144 | tf_op jit(solution)/shard_map/all_to_all | solution.py:48
  105.1 50.5 %all-to-all-start.1 = ((f32[64,2,512]{2,1,0:T(2,128)}), f32[64,2,512]{2,1,0:T(2,128)S(1)}, u32[]{:S(2)}, u32[]{:S(2)}) async-start(f32[64,2,512]{2,1,0:T(2,128)} %select_multiply_fusion), calls=%async_computation.1 | async-start | bytes 524288 | tf_op jit(solution)/shard_map/all_to_all | solution.py:141
  155.8 2.7 %copy-start.1 = (f32[16,64,64]{2,1,0:T(8,128)S(1)}, f32[16,64,64]{2,1,0:T(8,128)}, u32[]{:S(2)}) copy-start(f32[16,64,64]{2,1,0:T(8,128)} %param.17) | copy-start | bytes 786436
  155.8 4.0 %copy-start.2 = (f32[16,64,128]{2,1,0:T(8,128)S(1)}, f32[16,64,128]{2,1,0:T(8,128)}, u32[]{:S(2)}) copy-start(f32[16,64,128]{2,1,0:T(8,128)} %param.16) | copy-start | bytes 1572868
  156.6 3.2 %copy-start.6 = (f32[4,8,4,128]{3,1,2,0:T(8,128)S(1)}, f32[4,8,4,128]{3,1,2,0:T(8,128)}, u32[]{:S(2)}) copy-start(f32[4,8,4,128]{3,1,2,0:T(8,128)} %get-tuple-element.42) | copy-start | bytes 196612
where the time goes:
time: 162 us; the launch traced here: 161 us
  matrix products  47.7 us (29%)
  starting transfers between devices  45.5 us (28%)
  blocking collectives  37.2 us (23%)
  local copies, waits for them, and re-layouts  13.5 us (8%)
  waiting for transfers between devices  11.1 us (7%)
  other arithmetic  5.49 us (3%)
    all_gather x1, blocking collectives, one_gather(): lines, at, done = (lax.all_gather(ravelled, axis), 0, [])  37.2 us
    all_to_all x2, starting transfers between devices, sent_to_all(): return lax.all_to_all(copies, axis, split_axis=0, concat_axis=0, tiled=True)  23.9 us
    dot_general x4, matrix products, matern(): cross = jnp.einsum('dbp,dbkq->bkpq', left, right, precision=HIGHEST)  19.4 us
    dot_general x4, matrix products, one_block(): jnp.einsum('bkpq,sbkq->sbp', tile * live[:, :, None, None], weights, prec...  17.8 us
    ppermute x1, starting transfers between devices, padded(): lax.ppermute(first, axis, [(b, a) for a, b in up])  15 us
    all_to_all x2, waiting for transfers between devices, sent_to_all(): return lax.all_to_all(copies, axis, split_axis=0, concat_axis=0, tiled=True)  11.1 us
    all_to_all x1, starting transfers between devices, per_device(): lax.all_to_all(outgoing, 'leaf', split_axis=0, concat_axis=0, tiled=True)  4.8 us
  transfers between devices with their start and end apart: 5, of which 2 were waited for; matrix products, arithmetic and copies ran while one was open for 37% of the time, Pallas kernels for 0%

commit v1 on v0

v1 whole, which is shorter than its diff:
```python
import functools

import jax
import jax.numpy as jnp
from jax import lax
from jax.experimental import pallas as pl
from jax.experimental.pallas import tpu as pltpu
from jax.sharding import PartitionSpec as P

F32, BF16, I32 = jnp.float32, jnp.bfloat16, jnp.int32
MESH = pl.DeviceIdType.MESH


def iota(shape, dim):
    return lax.broadcasted_iota(I32, shape, dim)


def rounded(x):
    return x.astype(BF16).astype(F32)


def halves(x):
    high = x.astype(BF16)
    return high, (x - high.astype(F32)).astype(BF16)


def stack16(x):
    high = rounded(x)
    return jnp.concatenate([high, x - high], axis=0).astype(BF16)


def fold(x):
    return x[:8] + x[8:]


def nn(a, b):
    return lax.dot_general(a, b, (((1,), (0,)), ((), ())), preferred_element_type=F32)


def nt(a, b):
    return lax.dot_general(a, b, (((1,), (1,)), ((), ())), preferred_element_type=F32)


def split_dot(dot, x16, w):
    high, low = halves(w)
    return fold(dot(x16, high) + dot(x16, low))


def thirds(x):
    high = rounded(x)
    rest = x - high
    mid = rounded(rest)
    return high, mid, rest - mid


def norm_rows(norm, first):
    high, mid, low = thirds(norm)
    row = iota((32, norm.shape[1]), 0)
    at = row - first
    split = jnp.where(at == 0, high, jnp.where(at == 1, mid, jnp.where(at == 2, low, 0.0)))
    return jnp.where((row < 6) & ((at < 0) | (at > 2)), 1.0, split)


def kernel(
    side,
    n_grp,
    near_s,
    count_s,
    farc_s,
    pts_h,
    rhs_h,
    bases_h,
    upl_h,
    upc_h,
    cpl_h,
    cpc_h,
    cpg_h,
    farl_h,
    out_ref,
    st,
    bases_v,
    upl_v,
    upc_v,
    cpl_v,
    cpc_v,
    cpg_v,
    farl_v,
    bhi,
    blo,
    uhi,
    ulo,
    chi,
    clo,
    left_t,
    right,
    weight,
    coef2,
    near_out,
    down,
    tab_v,
    tab_s,
    ridx,
    reqz,
    reqy,
    ctz,
    cty,
    gcb,
    rows_out,
    rows_in,
    load_sem,
    tab_sem,
    st_send,
    st_recv,
    x_send,
    x_recv,
):
    n_leaf = side * side
    many = n_grp * n_leaf
    leaf_dev = bases_v.shape[0]
    grp, leaf = lax.axis_index("grp"), lax.axis_index("leaf")
    y, z = lax.div(leaf, side), lax.rem(leaf, side)
    dev = grp * n_leaf + leaf

    def at_dev(d):
        return lax.div(d, n_leaf), lax.rem(d, n_leaf)

    after, before = at_dev(lax.rem(dev + 1, many)), at_dev(lax.rem(dev + many - 1, many))

    barrier = pltpu.get_barrier_semaphore()

    def greet(who):
        pl.semaphore_signal(barrier, inc=1, device_id=who, device_id_type=MESH)

    greet(after)
    greet(before)

    def greet_leaf(j, c):
        greet((grp, lax.rem(leaf + j, n_leaf)))
        return c

    def greet_grp(j, c):
        greet((lax.rem(grp + j, n_grp), leaf))
        return c

    lax.fori_loop(1, n_leaf, greet_leaf, 0)
    lax.fori_loop(1, n_grp, greet_grp, 0)

    loads = {}
    plan = (
        ("farl", farl_h, farl_v),
        ("pts", pts_h, st.at[1, pl.ds(0, 16)]),
        ("rhs", rhs_h, st.at[1, pl.ds(16, 8)]),
        ("bases", bases_h, bases_v),
        ("upl", upl_h, upl_v),
        ("upc", upc_h, upc_v),
        ("cpl", cpl_h, cpl_v),
        ("cpc", cpc_h, cpc_v),
        ("cpg", cpg_h, cpg_v),
    )
    for i, (name, src, dst) in enumerate(plan):
        loads[name] = pltpu.make_async_copy(src, dst, load_sem.at[i])
        loads[name].start()

    def exchange(buf, at, peer, count, i):
        def go(j, c):
            pltpu.make_async_remote_copy(
                src_ref=buf.at[at],
                dst_ref=buf.at[at],
                send_sem=x_send.at[i],
                recv_sem=x_recv.at[i],
                device_id=peer(j),
                device_id_type=MESH,
            ).start()
            return c

        lax.fori_loop(1, count, go, 0)

    def arrived(ref, sem):
        pltpu.make_async_copy(ref, ref, sem).wait()

    def z_peer(j):
        return grp, y * side + lax.rem(z + j, side)

    def y_peer(j):
        return grp, lax.rem(y + j, side) * side + z

    def g_peer(j):
        return lax.rem(grp + j, n_grp), leaf

    loads["farl"].wait()
    far = farl_v[...]
    far_two = far.shape[1]
    lane, sub = iota((leaf_dev, 128), 1), iota((leaf_dev, 128), 0)
    wide = jnp.zeros((leaf_dev, 128), I32)
    for k in range(far_two):
        wide = jnp.where(lane == sub + leaf_dev * k, far[:, k : k + 1], wide)
    asks = leaf_dev * far_two
    row = jnp.sum(wide, axis=0, keepdims=True)
    row = jnp.where(iota((1, 128), 1) < asks, row, -1)
    reqz[z] = jnp.broadcast_to(row, (8, 128))
    owner = row >> 4
    lane_f, sub_f = iota((asks, 128), 1), iota((asks, 128), 0)
    spread = jnp.broadcast_to(owner.astype(F32), (asks, 128))
    column = jnp.sum(jnp.where(lane_f == sub_f, spread, 0.0), axis=1, keepdims=True)
    again = jnp.where((sub_f < lane_f) & (spread == column), 1.0, 0.0)
    again = jnp.max(again, axis=0, keepdims=True).astype(I32)
    place = ((leaf - (owner - grp * n_leaf)) & (n_leaf - 1)) - 1
    tab_v[...] = place * 2 + again
    tab_copy = pltpu.make_async_copy(tab_v, tab_s, tab_sem)
    tab_copy.start()

    loads["pts"].wait()
    loads["rhs"].wait()
    pl.semaphore_wait(barrier, n_leaf + n_grp)

    exchange(reqz, z, z_peer, side, 0)
    sides = []
    for i, (who, slot) in enumerate(((after, 0), (before, 2))):
        copy = pltpu.make_async_remote_copy(
            src_ref=st.at[1],
            dst_ref=st.at[slot],
            send_sem=st_send.at[i],
            recv_sem=st_recv.at[i],
            device_id=who,
            device_id_type=MESH,
        )
        copy.start()
        sides.append(copy)

    loads["bases"].wait()
    loads["upl"].wait()
    cc = jnp.zeros((16, 64), F32)
    for l in range(leaf_dev):
        x16 = stack16(st[1, 16:24, l * 128 : (l + 1) * 128])
        high, low = halves(bases_v[l])
        bhi[l], blo[l] = high, low
        two_high = jnp.concatenate([high, high], axis=0)
        two_low = jnp.concatenate([low, low], axis=0)
        c2 = fold(nt(x16, two_high) + nt(x16, two_low))
        coef2[l] = c2
        high, low = halves(upl_v[l])
        uhi[l], ulo[l] = high, low
        cc = cc + nn(stack16(c2), jnp.concatenate([high, low], axis=0))
    cc = fold(cc)
    loads["upc"].wait()
    term = split_dot(nn, stack16(cc), upc_v[0])
    ctz[z] = jnp.concatenate([cc, term], axis=1)
    exchange(ctz, z, z_peer, side, 1)

    arrived(reqz.at[pl.ds(0, side - 1)], x_recv.at[0])
    row8 = iota((8, 128), 0)
    tile = reqz[0]
    for i in range(1, side):
        tile = jnp.where(row8 == i, reqz[i], tile)
    reqy[y] = tile
    exchange(reqy, y, y_peer, side, 2)

    def features(block, m):
        a = st[block, 0:16, pl.ds(pl.multiple_of(m * 128, 128), 128)]
        return a, 0.75 * jnp.sum(a * a, axis=0, keepdims=True)

    def put_right(block, m, c):
        b, norm = features(block, m)
        high, mid, low = thirds(b)
        parts = [high, mid, high, mid, low, high, norm_rows(norm, 0)]
        right[block * leaf_dev + m] = jnp.concatenate(parts, axis=0).astype(BF16)
        x = st[block, 16:24, pl.ds(pl.multiple_of(m * 128, 128), 128)]
        top = rounded(x)
        first = jnp.concatenate([top, x - top], axis=0)
        second = jnp.concatenate([top, jnp.zeros_like(top)], axis=0)
        weight[block * leaf_dev + m] = jnp.concatenate([first, second], axis=1).astype(BF16)
        return c

    def put_left(l, c):
        a, norm = features(1, l)
        high, mid, low = thirds(-1.5 * a)
        parts = [high, high, mid, mid, high, low, norm_rows(norm, 3)]
        left_t[l] = jnp.concatenate(parts, axis=0).T.astype(BF16)
        return c

    lax.fori_loop(0, leaf_dev, put_left, 0)
    lax.fori_loop(0, leaf_dev, functools.partial(put_right, 1), 0)

    arrived(ctz.at[pl.ds(0, side - 1)], x_recv.at[1])
    low_lanes = iota((8, 128), 1) < 64
    total = ctz[0]
    for i in range(1, side):
        total = total + ctz[i]
    for i in range(side // 2):
        cty[y, i] = jnp.where(low_lanes, ctz[2 * i], pltpu.roll(ctz[2 * i + 1], 64, 1))
    cty[y, side // 2] = total
    exchange(cty, y, y_peer, side, 3)

    arrived(reqy.at[pl.ds(0, side - 1)], x_recv.at[2])
    lane8 = iota((8, 128), 1)
    for i in range(side):
        asked = reqy[i]
        mine = (asked >> 4) == dev
        code = (lane8 * 16 + (asked & 15)).astype(F32)
        first = jnp.min(jnp.where(mine, code, 4096.0), axis=1, keepdims=True)
        last = jnp.max(jnp.where(mine, code, 0.0), axis=1, keepdims=True)
        ridx[i * 8 : (i + 1) * 8] = jnp.where(low_lanes, first, last).astype(I32) & 15

    def send_row(j, c):
        who = lax.rem(leaf + j, n_leaf)
        index = jnp.broadcast_to(ridx[pl.ds(who, 1), :], (8, 128))
        picked = coef2[0]
        for l in range(1, leaf_dev):
            picked = jnp.where(index == l, coef2[l], picked)
        rows_out[j - 1] = picked
        pltpu.make_async_remote_copy(
            src_ref=rows_out.at[j - 1],
            dst_ref=rows_in.at[j - 1],
            send_sem=x_send.at[5],
            recv_sem=x_recv.at[5],
            device_id=(grp, who),
            device_id_type=MESH,
        ).start()
        return c

    lax.fori_loop(1, n_leaf, send_row, 0)

    loads["cpl"].wait()

    def put_coupling(l, c):
        parts = [cpl_v[l, k] for k in range(far_two)]
        high, low = halves(jnp.concatenate(parts, axis=1))
        chi[l], clo[l] = high, low
        return c

    lax.fori_loop(0, leaf_dev, put_coupling, 0)

    arrived(cty.at[pl.ds(0, side - 1)], x_recv.at[3])
    total = cty[0, side // 2]
    for i in range(1, side):
        total = total + cty[i, side // 2]
    gcb[grp] = total
    exchange(gcb, grp, g_peer, n_grp, 4)

    for copy in sides:
        copy.wait_recv()
    lax.fori_loop(0, leaf_dev, functools.partial(put_right, 0), 0)
    lax.fori_loop(0, leaf_dev, functools.partial(put_right, 2), 0)
    slots = near_s.shape[1]
    base = (dev - 1) * leaf_dev

    def near_leaf(l, c):
        lhs = left_t[l]
        count = count_s[l]
        acc = jnp.zeros((16, 128), F32)
        for k in range(slots):
            m = jnp.clip(near_s[l, k] - base, 0, 3 * leaf_dev - 1)
            gap = jnp.maximum(nn(lhs, right[m]), 1e-30)
            u = gap * lax.rsqrt(gap)
            value = (1.0 + u) * jnp.exp(-u)
            high = value.astype(BF16)
            low = (value - high.astype(F32)).astype(BF16)
            live = jnp.where(k < count, 1.0, 0.0).astype(F32)
            part = nt(weight[m], jnp.concatenate([high, low], axis=1))
            acc = acc + live * part
        near_out[l] = fold(acc)
        return c

    lax.fori_loop(0, leaf_dev, near_leaf, 0)

    arrived(gcb.at[pl.ds(0, n_grp - 1)], x_recv.at[4])
    loads["cpc"].wait()
    loads["cpg"].wait()
    field_group = jnp.zeros((8, 64), F32)
    for h in range(n_grp):
        other = jnp.where(grp == h, 0.0, 1.0).astype(F32)
        gc = gcb[h][:, 64:] * other
        field_group = field_group + split_dot(nt, stack16(gc), cpg_v[0, h])
    field_cluster = split_dot(nt, stack16(field_group), upc_v[0])
    for k in range(cpc_v.shape[1]):
        f = jnp.clip(farc_s[0, k] - grp * n_leaf, 0, n_leaf - 1)
        fy, fz = lax.div(f, side), lax.rem(f, side)
        pair = cty[fy, lax.div(fz, 2)]
        flag = jnp.full((8, 128), lax.rem(fz, 2), I32)
        one = jnp.where(flag == 1, pltpu.roll(pair, 64, 1), pair)[:, :64]
        field_cluster = field_cluster + split_dot(nt, stack16(one), cpc_v[0, k])
    fc16 = stack16(field_cluster)
    for l in range(leaf_dev):
        down[l] = fold(nt(fc16, uhi[l]) + nt(fc16, ulo[l]))

    arrived(rows_in, x_recv.at[5])
    tab_copy.wait()
    for l in range(leaf_dev):
        chunks = []
        for pair in range(far_two // 2):
            both = []
            for half in range(2):
                t = tab_s[0, (2 * pair + half) * leaf_dev + l]
                got = rows_in[jnp.clip(t >> 1, 0, n_leaf - 2)]
                flag = jnp.full((8, 128), t & 1, I32)
                both.append(jnp.where(flag == half, got, pltpu.roll(got, 64, 1)))
            chunks.append(jnp.where(low_lanes, both[0], both[1]))
        x16 = stack16(jnp.concatenate(chunks, axis=1))
        field = fold(nt(x16, chi[l]) + nt(x16, clo[l])) + down[l]
        f16 = stack16(field)
        out_ref[:, l * 128 : (l + 1) * 128] = fold(nn(f16, bhi[l]) + nn(f16, blo[l])) + near_out[l]

    for copy in sides:
        copy.wait_send()
    for i, buf, n in ((0, reqz, side), (1, ctz, side), (2, reqy, side), (3, cty, side), (4, gcb, n_grp)):
        arrived(buf.at[pl.ds(0, n - 1)], x_send.at[i])
    arrived(rows_out, x_send.at[5])


def per_device(
    points,
    rhs,
    bases,
    up_leaf,
    up_cluster,
    coupling_leaf,
    coupling_cluster,
    coupling_group,
    near_list,
    near_count,
    far_leaf,
    far_cluster,
):
    n_leaf, n_grp = lax.axis_size("leaf"), lax.axis_size("grp")
    side = round(n_leaf**0.5)
    leaf_dev, rank, width = bases.shape
    nrhs = rhs.shape[0]
    far_two = far_leaf.shape[1]
    anywhere = pl.BlockSpec(memory_space=pl.ANY)
    scalars = pl.BlockSpec(memory_space=pltpu.SMEM)
    vmem = pltpu.VMEM
    return pl.pallas_call(
        functools.partial(kernel, side, n_grp),
        out_shape=jax.ShapeDtypeStruct(rhs.shape, F32),
        in_specs=[scalars] * 3 + [anywhere] * 9,
        out_specs=pl.BlockSpec(memory_space=vmem),
        scratch_shapes=[
            vmem((3, 24, points.shape[1]), F32),
            vmem(bases.shape, F32),
            vmem(up_leaf.shape, F32),
            vmem(up_cluster.shape, F32),
            vmem(coupling_leaf.shape, F32),
            vmem(coupling_cluster.shape, F32),
            vmem(coupling_group.shape, F32),
            vmem(far_leaf.shape, I32),
            vmem(bases.shape, BF16),
            vmem(bases.shape, BF16),
            vmem(up_leaf.shape, BF16),
            vmem(up_leaf.shape, BF16),
            vmem((leaf_dev, rank, far_two * rank), BF16),
            vmem((leaf_dev, rank, far_two * rank), BF16),
            vmem((leaf_dev, width, 128), BF16),
            vmem((3 * leaf_dev, 128, width), BF16),
            vmem((3 * leaf_dev, 16, 2 * width), BF16),
            vmem((leaf_dev, nrhs, 128), F32),
            vmem((leaf_dev, nrhs, width), F32),
            vmem((leaf_dev, nrhs, rank), F32),
            vmem((1, 128), I32),
            pltpu.SMEM((1, 128), I32),
            vmem((n_leaf, 128), I32),
            vmem((side, 8, 128), I32),
            vmem((side, 8, 128), I32),
            vmem((side, 8, 128), F32),
            vmem((side, side // 2 + 1, 8, 128), F32),
            vmem((n_grp, 8, 128), F32),
            vmem((n_leaf - 1, 8, 128), F32),
            vmem((n_leaf - 1, 8, 128), F32),
            pltpu.SemaphoreType.DMA((9,)),
            pltpu.SemaphoreType.DMA,
            pltpu.SemaphoreType.DMA((2,)),
            pltpu.SemaphoreType.DMA((2,)),
            pltpu.SemaphoreType.DMA((6,)),
            pltpu.SemaphoreType.DMA((6,)),
        ],
        compiler_params=pltpu.CompilerParams(
            collective_id=0, has_side_effects=True, vmem_limit_bytes=32 * 1024 * 1024
        ),
    )(
        near_list,
        near_count,
        far_cluster,
        points,
        rhs,
        bases,
        up_leaf,
        up_cluster,
        coupling_leaf,
        coupling_cluster,
        coupling_group,
        far_leaf,
    )


def solution(mesh):
    placed = (
        P(None, ("grp", "leaf")),
        P(None, ("grp", "leaf")),
        P(("grp", "leaf"), None, None),
        P(("grp", "leaf"), None, None),
        P(("grp", "leaf"), None, None),
        P(("grp", "leaf"), None, None, None),
        P(("grp", "leaf"), None, None, None),
        P("grp", None, None, None),
        P(("grp", "leaf"), None),
        P(("grp", "leaf")),
        P(("grp", "leaf"), None),
        P(("grp", "leaf"), None),
    )
    return jax.shard_map(
        per_device, mesh=mesh, in_specs=placed, out_specs=P(None, ("grp", "leaf")), check_vma=False
    )
```

time: 162 us -> 63.7 us (0.39)
  the two profiles are of different devices: /device:TPU:1 before, /device:TPU:2 now
where the time goes in v1:
time: 63.7 us; the launch traced here: 63.2 us
  Pallas kernels  51.7 us (81%)
  local copies, waits for them, and re-layouts  11.5 us (18%)
    pallas_call x1, Pallas kernels, per_device(): pl.pallas_call(functools.partial(kernel, side, n_grp), out_shape=jax.Shap...  51.7 us
    unnamed x23, local copies, waits for them, and re-layouts  11.5 us

profile of v1, /device:TPU:2, one launch (start us, length us, event | category | flops | bytes accessed | tf_op | source)
XLA Modules:
  0.0 63.2 jit_solution(15758649195513526385)
XLA Ops:
  0.0 0.8 %copy.13.near_s = s32[16,8]{1,0:T(8,128)S(1)} copy(s32[16,8]{0,1:T(8,128)} %param.20) | data formatting | bytes 1024 | tf_op args[8]
  0.8 0.8 %copy.14.farl_h = s32[16,4]{1,0:T(8,128)S(1)} copy(s32[16,4]{0,1:T(4,128)} %param.22) | data formatting | bytes 512 | tf_op args[10]
  1.5 0.0 copy-start
  1.5 1.6 %copy-done = f32[16,4,64,64]{3,2,1,0:T(8,128)S(1)} copy-done((f32[16,4,64,64]{3,2,1,0:T(8,128)S(1)}, f32[16,4,64,64]{3,2,1,0:T(8,128)}, u32[]{:S(2)}) %copy-start) | copy-done | bytes 1048600
  3.1 0.0 copy-start.1
  3.1 1.0 %copy-done.1 = f32[16,64,128]{2,1,0:T(8,128)S(1)} copy-done((f32[16,64,128]{2,1,0:T(8,128)S(1)}, f32[16,64,128]{2,1,0:T(8,128)}, u32[]{:S(2)}) %copy-start.1) | copy-done | bytes 524312
  4.1 0.0 copy-start.2
  4.2 1.0 %copy-done.2 = f32[16,64,64]{2,1,0:T(8,128)S(1)} copy-done((f32[16,64,64]{2,1,0:T(8,128)S(1)}, f32[16,64,64]{2,1,0:T(8,128)}, u32[]{:S(2)}) %copy-start.2) | copy-done | bytes 262168
  5.2 0.0 copy-start.3
  5.2 0.9 %copy-done.3 = f32[1,8,64,64]{3,2,1,0:T(8,128)S(1)} copy-done((f32[1,8,64,64]{3,2,1,0:T(8,128)S(1)}, f32[1,8,64,64]{3,2,1,0:T(8,128)}, u32[]{:S(2)}) %copy-start.3) | copy-done | bytes 131096
  6.1 0.0 copy-start.4
  6.1 0.9 %copy-done.4 = f32[16,2048]{1,0:T(8,128)S(1)} copy-done((f32[16,2048]{1,0:T(8,128)S(1)}, f32[16,2048]{1,0:T(8,128)}, u32[]{:S(2)}) %copy-start.4) | copy-done | bytes 131096
  7.0 0.0 copy-start.5
  7.0 0.9 %copy-done.5 = f32[1,4,64,64]{3,2,1,0:T(8,128)S(1)} copy-done((f32[1,4,64,64]{3,2,1,0:T(8,128)S(1)}, f32[1,4,64,64]{3,2,1,0:T(8,128)}, u32[]{:S(2)}) %copy-start.5) | copy-done | bytes 65560
  8.0 0.0 copy-start.6
  8.0 0.8 %copy-done.6 = f32[8,2048]{1,0:T(8,128)S(1)} copy-done((f32[8,2048]{1,0:T(8,128)S(1)}, f32[8,2048]{1,0:T(8,128)}, u32[]{:S(2)}) %copy-start.6) | copy-done | bytes 65560
  8.8 0.0 copy-start.7
  8.8 0.8 %copy-done.7 = f32[1,64,64]{2,1,0:T(8,128)S(1)} copy-done((f32[1,64,64]{2,1,0:T(8,128)S(1)}, f32[1,64,64]{2,1,0:T(8,128)}, u32[]{:S(2)}) %copy-start.7) | copy-done | bytes 16408
  9.6 0.0 copy-start.8
  9.6 0.7 %copy-done.8 = s32[16]{0:T(128)S(1)} copy-done((s32[16]{0:T(128)S(1)}, s32[16]{0:T(128)}, u32[]{:S(2)}) %copy-start.8) | copy-done | bytes 88
  10.2 0.0 copy-start.9
  10.2 0.7 %copy-done.9 = s32[1,4]{1,0:T(1,128)S(1)} copy-done((s32[1,4]{1,0:T(1,128)S(1)}, s32[1,4]{1,0:T(1,128)}, u32[]{:S(2)}) %copy-start.9) | copy-done | bytes 40
  10.9 51.7 %shard_map.118 = f32[8,2048]{1,0:T(8,128)S(1)} custom-call(s32[16,8]{1,0:T(8,128)S(1)} %copy.13.near_s, s32[16]{0:T(128)S(1)} %copy-done.8, s32[1,4]{1,0:T(1,128)S(1)} %copy-done.9, f32[16,2048]{1,0:T(8,128)S(1)} %copy-done.4, f32[8,2048]{1,0:T(8,128)S(1)} %copy-done.6, f32[16,64,128]{2,1,0:T(8,128)S(1)} %copy-done.1, f32[16,64,64]{2,1,0:T(8,128)S(1)} %copy-done.2, ...), custom_call_target="tpu_custom_call" | custom-call | tf_op jit(solution)/shard_map/pallas_call | solution.py:432
  62.6 0.6 copy.16
Async XLA Ops:
  1.5 1.6 %copy-start = (f32[16,4,64,64]{3,2,1,0:T(8,128)S(1)}, f32[16,4,64,64]{3,2,1,0:T(8,128)}, u32[]{:S(2)}) copy-start(f32[16,4,64,64]{3,2,1,0:T(8,128)} %cpl_h.1) | copy-start | bytes 3145732
  3.1 1.0 %copy-start.1 = (f32[16,64,128]{2,1,0:T(8,128)S(1)}, f32[16,64,128]{2,1,0:T(8,128)}, u32[]{:S(2)}) copy-start(f32[16,64,128]{2,1,0:T(8,128)} %bases_h.1) | copy-start | bytes 1572868
  4.1 1.0 %copy-start.2 = (f32[16,64,64]{2,1,0:T(8,128)S(1)}, f32[16,64,64]{2,1,0:T(8,128)}, u32[]{:S(2)}) copy-start(f32[16,64,64]{2,1,0:T(8,128)} %upl_h.1) | copy-start | bytes 786436
  5.2 0.9 %copy-start.3 = (f32[1,8,64,64]{3,2,1,0:T(8,128)S(1)}, f32[1,8,64,64]{3,2,1,0:T(8,128)}, u32[]{:S(2)}) copy-start(f32[1,8,64,64]{3,2,1,0:T(8,128)} %cpg_h.1) | copy-start | bytes 393220
  6.1 0.9 %copy-start.4 = (f32[16,2048]{1,0:T(8,128)S(1)}, f32[16,2048]{1,0:T(8,128)}, u32[]{:S(2)}) copy-start(f32[16,2048]{1,0:T(8,128)} %pts_h.1) | copy-start | bytes 393220
  7.0 0.9 %copy-start.5 = (f32[1,4,64,64]{3,2,1,0:T(8,128)S(1)}, f32[1,4,64,64]{3,2,1,0:T(8,128)}, u32[]{:S(2)}) copy-start(f32[1,4,64,64]{3,2,1,0:T(8,128)} %cpc_h.1) | copy-start | bytes 196612
  8.0 0.8 %copy-start.6 = (f32[8,2048]{1,0:T(8,128)S(1)}, f32[8,2048]{1,0:T(8,128)}, u32[]{:S(2)}) copy-start(f32[8,2048]{1,0:T(8,128)} %rhs_h.1) | copy-start | bytes 196612
  8.8 0.8 %copy-start.7 = (f32[1,64,64]{2,1,0:T(8,128)S(1)}, f32[1,64,64]{2,1,0:T(8,128)}, u32[]{:S(2)}) copy-start(f32[1,64,64]{2,1,0:T(8,128)} %upc_h.1) | copy-start | bytes 49156
  9.6 0.7 %copy-start.8 = (s32[16]{0:T(128)S(1)}, s32[16]{0:T(128)}, u32[]{:S(2)}) copy-start(s32[16]{0:T(128)} %count_s.1) | copy-start | bytes 196
  10.2 0.7 %copy-start.9 = (s32[1,4]{1,0:T(1,128)S(1)}, s32[1,4]{1,0:T(1,128)}, u32[]{:S(2)}) copy-start(s32[1,4]{1,0:T(1,128)} %farc_s.1) | copy-start | bytes 52

commit v2 on v1

--- a/solution.py
+++ b/solution.py
@@ -9,6 +9,15 @@
 
 F32, BF16, I32 = jnp.float32, jnp.bfloat16, jnp.int32
 MESH = pl.DeviceIdType.MESH
+
+
+def loop(start, stop, step, body):
+    def some(i, c):
+        for j in range(step):
+            body(start + i * step + j)
+        return c
+
+    lax.fori_loop(0, (stop - start) // step, some, 0)
 
 
 def iota(shape, dim):
@@ -91,7 +100,7 @@
     ulo,
     chi,
     clo,
-    left_t,
+    left,
     right,
     weight,
     coef2,
@@ -126,25 +135,6 @@
 
     after, before = at_dev(lax.rem(dev + 1, many)), at_dev(lax.rem(dev + many - 1, many))
 
-    barrier = pltpu.get_barrier_semaphore()
-
-    def greet(who):
-        pl.semaphore_signal(barrier, inc=1, device_id=who, device_id_type=MESH)
-
-    greet(after)
-    greet(before)
-
-    def greet_leaf(j, c):
-        greet((grp, lax.rem(leaf + j, n_leaf)))
-        return c
-
-    def greet_grp(j, c):
-        greet((lax.rem(grp + j, n_grp), leaf))
-        return c
-
-    lax.fori_loop(1, n_leaf, greet_leaf, 0)
-    lax.fori_loop(1, n_grp, greet_grp, 0)
-
     loads = {}
     plan = (
         ("farl", farl_h, farl_v),
@@ -161,8 +151,19 @@
         loads[name] = pltpu.make_async_copy(src, dst, load_sem.at[i])
         loads[name].start()
 
+    barrier = pltpu.get_barrier_semaphore()
+
+    def greet(who):
+        pl.semaphore_signal(barrier, inc=1, device_id=who, device_id_type=MESH)
+
+    greet(after)
+    greet(before)
+
+    loop(1, n_leaf, 7, lambda j: greet((grp, lax.rem(leaf + j, n_leaf))))
+    loop(1, n_grp, 7, lambda j: greet((lax.rem(grp + j, n_grp), leaf)))
+
     def exchange(buf, at, peer, count, i):
-        def go(j, c):
+        def go(j):
             pltpu.make_async_remote_copy(
                 src_ref=buf.at[at],
                 dst_ref=buf.at[at],
@@ -171,9 +172,8 @@
                 device_id=peer(j),
                 device_id_type=MESH,
             ).start()
-            return c
-
-        lax.fori_loop(1, count, go, 0)
+
+        loop(1, count, 7, go)
 
     def arrived(ref, sem):
         pltpu.make_async_copy(ref, ref, sem).wait()
@@ -189,14 +189,10 @@
 
     loads["farl"].wait()
     far = farl_v[...]
-    far_two = far.shape[1]
-    lane, sub = iota((leaf_dev, 128), 1), iota((leaf_dev, 128), 0)
-    wide = jnp.zeros((leaf_dev, 128), I32)
-    for k in range(far_two):
-        wide = jnp.where(lane == sub + leaf_dev * k, far[:, k : k + 1], wide)
+    far_two = far.shape[0]
     asks = leaf_dev * far_two
-    row = jnp.sum(wide, axis=0, keepdims=True)
-    row = jnp.where(iota((1, 128), 1) < asks, row, -1)
+    parts = [far[k : k + 1] for k in range(far_two)]
+    row = jnp.concatenate([*parts, jnp.full((1, 128 - asks), -1, I32)], axis=1)
     reqz[z] = jnp.broadcast_to(row, (8, 128))
     owner = row >> 4
     lane_f, sub_f = iota((asks, 128), 1), iota((asks, 128), 0)
@@ -259,27 +255,25 @@
         a = st[block, 0:16, pl.ds(pl.multiple_of(m * 128, 128), 128)]
         return a, 0.75 * jnp.sum(a * a, axis=0, keepdims=True)
 
-    def put_right(block, m, c):
+    def put_right(block, m):
         b, norm = features(block, m)
         high, mid, low = thirds(b)
         parts = [high, mid, high, mid, low, high, norm_rows(norm, 0)]
-        right[block * leaf_dev + m] = jnp.concatenate(parts, axis=0).astype(BF16)
+        right[block * leaf_dev + m] = jnp.concatenate(parts, axis=0).T.astype(BF16)
         x = st[block, 16:24, pl.ds(pl.multiple_of(m * 128, 128), 128)]
         top = rounded(x)
         first = jnp.concatenate([top, x - top], axis=0)
         second = jnp.concatenate([top, jnp.zeros_like(top)], axis=0)
         weight[block * leaf_dev + m] = jnp.concatenate([first, second], axis=1).astype(BF16)
-        return c
-
-    def put_left(l, c):
+
+    def put_left(l):
         a, norm = features(1, l)
         high, mid, low = thirds(-1.5 * a)
         parts = [high, high, mid, mid, high, low, norm_rows(norm, 3)]
-        left_t[l] = jnp.concatenate(parts, axis=0).T.astype(BF16)
-        return c
-
-    lax.fori_loop(0, leaf_dev, put_left, 0)
-    lax.fori_loop(0, leaf_dev, functools.partial(put_right, 1), 0)
+        left[l] = jnp.concatenate(parts, axis=0).astype(BF16)
+
+    loop(0, leaf_dev, 4, put_left)
+    loop(0, leaf_dev, 4, functools.partial(put_right, 1))
 
     arrived(ctz.at[pl.ds(0, side - 1)], x_recv.at[1])
     low_lanes = iota((8, 128), 1) < 64
@@ -301,7 +295,7 @@
         last = jnp.max(jnp.where(mine, code, 0.0), axis=1, keepdims=True)
         ridx[i * 8 : (i + 1) * 8] = jnp.where(low_lanes, first, last).astype(I32) & 15
 
-    def send_row(j, c):
+    def send_row(j):
         who = lax.rem(leaf + j, n_leaf)
         index = jnp.broadcast_to(ridx[pl.ds(who, 1), :], (8, 128))
         picked = coef2[0]
@@ -316,19 +310,17 @@
             device_id=(grp, who),
             device_id_type=MESH,
         ).start()
-        return c
-
-    lax.fori_loop(1, n_leaf, send_row, 0)
+
+    loop(1, n_leaf, 7, send_row)
 
     loads["cpl"].wait()
 
-    def put_coupling(l, c):
+    def put_coupling(l):
         parts = [cpl_v[l, k] for k in range(far_two)]
         high, low = halves(jnp.concatenate(parts, axis=1))
         chi[l], clo[l] = high, low
-        return c
-
-    lax.fori_loop(0, leaf_dev, put_coupling, 0)
+
+    loop(0, leaf_dev, 4, put_coupling)
 
     arrived(cty.at[pl.ds(0, side - 1)], x_recv.at[3])
     total = cty[0, side // 2]
@@ -337,31 +329,29 @@
     gcb[grp] = total
     exchange(gcb, grp, g_peer, n_grp, 4)
 
-    for copy in sides:
+    for copy, block in zip(sides, (0, 2)):
         copy.wait_recv()
-    lax.fori_loop(0, leaf_dev, functools.partial(put_right, 0), 0)
-    lax.fori_loop(0, leaf_dev, functools.partial(put_right, 2), 0)
-    slots = near_s.shape[1]
+        loop(0, leaf_dev, 4, functools.partial(put_right, block))
+    slots = near_s.shape[0]
     base = (dev - 1) * leaf_dev
 
-    def near_leaf(l, c):
-        lhs = left_t[l]
+    def near_leaf(l):
+        target = left[l]
         count = count_s[l]
         acc = jnp.zeros((16, 128), F32)
         for k in range(slots):
-            m = jnp.clip(near_s[l, k] - base, 0, 3 * leaf_dev - 1)
-            gap = jnp.maximum(nn(lhs, right[m]), 1e-30)
+            m = jnp.clip(near_s[k, l] - base, 0, 3 * leaf_dev - 1)
+            gap = jnp.maximum(nn(right[m], target), 1e-30)
             u = gap * lax.rsqrt(gap)
             value = (1.0 + u) * jnp.exp(-u)
             high = value.astype(BF16)
             low = (value - high.astype(F32)).astype(BF16)
             live = jnp.where(k < count, 1.0, 0.0).astype(F32)
-            part = nt(weight[m], jnp.concatenate([high, low], axis=1))
+            part = nn(weight[m], jnp.concatenate([high, low], axis=0))
             acc = acc + live * part
         near_out[l] = fold(acc)
-        return c
-
-    lax.fori_loop(0, leaf_dev, near_leaf, 0)
+
+    loop(0, leaf_dev, 4, near_leaf)
 
     arrived(gcb.at[pl.ds(0, n_grp - 1)], x_recv.at[4])
     loads["cpc"].wait()
@@ -426,12 +416,12 @@
     leaf_dev, rank, width = bases.shape
     nrhs = rhs.shape[0]
     far_two = far_leaf.shape[1]
-    anywhere = pl.BlockSpec(memory_space=pl.ANY)
+    anywhere = pl.BlockSpec(memory_space=pltpu.HBM)
     scalars = pl.BlockSpec(memory_space=pltpu.SMEM)
     vmem = pltpu.VMEM
     return pl.pallas_call(
         functools.partial(kernel, side, n_grp),
-        out_shape=jax.ShapeDtypeStruct(rhs.shape, F32),
+        out_shape=vmem(rhs.shape, F32),
         in_specs=[scalars] * 3 + [anywhere] * 9,
         out_specs=pl.BlockSpec(memory_space=vmem),
         scratch_shapes=[
@@ -442,7 +432,7 @@
             vmem(coupling_leaf.shape, F32),
             vmem(coupling_cluster.shape, F32),
             vmem(coupling_group.shape, F32),
-            vmem(far_leaf.shape, I32),
+            vmem(far_leaf.shape[::-1], I32),
             vmem(bases.shape, BF16),
             vmem(bases.shape, BF16),
             vmem(up_leaf.shape, BF16),
@@ -476,18 +466,23 @@
             collective_id=0, has_side_effects=True, vmem_limit_bytes=32 * 1024 * 1024
         ),
     )(
-        near_list,
-        near_count,
-        far_cluster,
-        points,
-        rhs,
-        bases,
-        up_leaf,
-        up_cluster,
-        coupling_leaf,
-        coupling_cluster,
-        coupling_group,
-        far_leaf,
+        *(
+            pltpu.with_memory_space_constraint(a, pltpu.HBM)
+            for a in (
+                near_list.T,
+                near_count,
+                far_cluster,
+                points,
+                rhs,
+                bases,
+                up_leaf,
+                up_cluster,
+                coupling_leaf,
+                coupling_cluster,
+                coupling_group,
+                far_leaf.T,
+            )
+        )
     )
 
 

time: 63.7 us -> 42 us (0.66)
  the two profiles are of different devices: /device:TPU:2 before, /device:TPU:1 now
where the time goes in v2:
time: 42 us; the launch traced here: 41.8 us
  Pallas kernels  41.2 us (98%)
  local copies, waits for them, and re-layouts  0.63 us (2%)
    pallas_call x1, Pallas kernels, per_device(): pl.pallas_call(functools.partial(kernel, side, n_grp), out_shape=vmem(rhs...  41.2 us

profile of v2, /device:TPU:1, one launch (start us, length us, event | category | flops | bytes accessed | tf_op | source)
XLA Modules:
  0.0 41.8 jit_solution(14914285952050593192)
XLA Ops:
  0.0 41.2 %shard_map.118 = f32[8,2048]{1,0:T(8,128)S(1)} custom-call(s32[8,16]{1,0:T(8,128)} %bitcast.2, s32[16]{0:T(128)} %count_s.1, s32[1,4]{1,0:T(1,128)} %farc_s.1, f32[16,2048]{1,0:T(8,128)} %pts_h.1, f32[8,2048]{1,0:T(8,128)} %rhs_h.1, f32[16,64,128]{2,1,0:T(8,128)} %bases_h.1, f32[16,64,64]{2,1,0:T(8,128)} %upl_h.1, f32[1,64,64]{2,1,0:T(8,128)} %upc_h.1, ...), custom_call_target="tpu_custom_call" | custom-call | tf_op jit(solution)/shard_map/pallas_call | solution.py:422
  41.2 0.6 %copy.14 = f32[8,2048]{1,0:T(8,128)} copy(f32[8,2048]{1,0:T(8,128)S(1)} %shard_map.118) | data formatting | bytes 131072

commit v3 on v2

--- a/solution.py
+++ b/solution.py
@@ -73,9 +73,9 @@
 def kernel(
     side,
     n_grp,
-    near_s,
-    count_s,
-    farc_s,
+    near_h,
+    count_h,
+    farc_h,
     pts_h,
     rhs_h,
     bases_h,
@@ -86,6 +86,9 @@
     cpg_h,
     farl_h,
     out_ref,
+    near_s,
+    count_s,
+    farc_s,
     st,
     bases_v,
     upl_v,
@@ -96,21 +99,24 @@
     farl_v,
     bhi,
     blo,
-    uhi,
-    ulo,
-    chi,
-    clo,
+    vhi,
+    vlo,
+    whi,
+    wlo,
+    ghi,
+    glo,
     left,
     right,
     weight,
     coef2,
     near_out,
     down,
+    near_fc,
     tab_v,
     tab_s,
     ridx,
-    reqz,
-    reqy,
+    ask,
+    asked_by,
     ctz,
     cty,
     gcb,
@@ -135,6 +141,17 @@
 
     after, before = at_dev(lax.rem(dev + 1, many)), at_dev(lax.rem(dev + many - 1, many))
 
+    barrier = pltpu.get_barrier_semaphore()
+
+    def greet(who):
+        pl.semaphore_signal(barrier, inc=1, device_id=who, device_id_type=MESH)
+
+    greet(after)
+    greet(before)
+
+    loop(1, n_leaf, 7, lambda j: greet((grp, lax.rem(leaf + j, n_leaf))))
+    loop(1, n_grp, 7, lambda j: greet((lax.rem(grp + j, n_grp), leaf)))
+
     loads = {}
     plan = (
         ("farl", farl_h, farl_v),
@@ -146,21 +163,13 @@
         ("cpl", cpl_h, cpl_v),
         ("cpc", cpc_h, cpc_v),
         ("cpg", cpg_h, cpg_v),
+        ("near", near_h, near_s),
+        ("count", count_h, count_s),
+        ("farc", farc_h, farc_s),
     )
     for i, (name, src, dst) in enumerate(plan):
         loads[name] = pltpu.make_async_copy(src, dst, load_sem.at[i])
         loads[name].start()
-
-    barrier = pltpu.get_barrier_semaphore()
-
-    def greet(who):
-        pl.semaphore_signal(barrier, inc=1, device_id=who, device_id_type=MESH)
-
-    greet(after)
-    greet(before)
-
-    loop(1, n_leaf, 7, lambda j: greet((grp, lax.rem(leaf + j, n_leaf))))
-    loop(1, n_grp, 7, lambda j: greet((lax.rem(grp + j, n_grp), leaf)))
 
     def exchange(buf, at, peer, count, i):
         def go(j):
@@ -193,7 +202,8 @@
     asks = leaf_dev * far_two
     parts = [far[k : k + 1] for k in range(far_two)]
     row = jnp.concatenate([*parts, jnp.full((1, 128 - asks), -1, I32)], axis=1)
-    reqz[z] = jnp.broadcast_to(row, (8, 128))
+    ask[...] = row
+    asked_by[pl.ds(leaf, 1)] = jnp.full((1, 128), -1, I32)
     owner = row >> 4
     lane_f, sub_f = iota((asks, 128), 1), iota((asks, 128), 0)
     spread = jnp.broadcast_to(owner.astype(F32), (asks, 128))
@@ -205,11 +215,63 @@
     tab_copy = pltpu.make_async_copy(tab_v, tab_s, tab_sem)
     tab_copy.start()
 
+    loads["rhs"].wait()
+    loads["bases"].wait()
+    loads["upl"].wait()
+    cc = jnp.zeros((16, 64), F32)
+    for l in range(leaf_dev):
+        x16 = stack16(st[1, 16:24, l * 128 : (l + 1) * 128])
+        high, low = halves(bases_v[l])
+        bhi[l], blo[l] = high, low
+        two_high = jnp.concatenate([high, high], axis=0)
+        two_low = jnp.concatenate([low, low], axis=0)
+        c2 = fold(nt(x16, two_high) + nt(x16, two_low))
+        coef2[l] = c2
+        high, low = halves(upl_v[l])
+        cc = cc + nn(stack16(c2), jnp.concatenate([high, low], axis=0))
+    cc = fold(cc)
+    loads["upc"].wait()
+    term = split_dot(nn, stack16(cc), upc_v[0])
+    ctz[z] = jnp.concatenate([cc, term], axis=1)
+
     loads["pts"].wait()
-    loads["rhs"].wait()
     pl.semaphore_wait(barrier, n_leaf + n_grp)
 
-    exchange(reqz, z, z_peer, side, 0)
+    def send_ask(j):
+        pltpu.make_async_remote_copy(
+            src_ref=ask,
+            dst_ref=asked_by.at[pl.ds(leaf, 1)],
+            send_sem=x_send.at[0],
+            recv_sem=x_recv.at[0],
+            device_id=(grp, lax.rem(leaf + j, n_leaf)),
+            device_id_type=MESH,
+        ).start()
+
+    exchange(ctz, z, z_peer, side, 1)
+    loop(1, n_leaf, 7, send_ask)
+    def features(block, m):
+        a = st[block, 0:16, pl.ds(pl.multiple_of(m * 128, 128), 128)]
+        return a, 0.75 * jnp.sum(a * a, axis=0, keepdims=True)
+
+    def put_right(block, m):
+        b, norm = features(block, m)
+        high, mid, low = thirds(b)
+        parts = [high, mid, high, mid, low, high, norm_rows(norm, 0)]
+        right[block * leaf_dev + m] = jnp.concatenate(parts, axis=0).T.astype(BF16)
+        x = st[block, 16:24, pl.ds(pl.multiple_of(m * 128, 128), 128)]
+        top = rounded(x)
+        first = jnp.concatenate([top, x - top], axis=0)
+        second = jnp.concatenate([top, jnp.zeros_like(top)], axis=0)
+        weight[block * leaf_dev + m] = jnp.concatenate([first, second], axis=1).astype(BF16)
+
+    def put_left(l):
+        a, norm = features(1, l)
+        high, mid, low = thirds(-1.5 * a)
+        parts = [high, high, mid, mid, high, low, norm_rows(norm, 3)]
+        left[l] = jnp.concatenate(parts, axis=0).astype(BF16)
+
+    loop(0, leaf_dev, 4, put_left)
+    loop(0, leaf_dev, 4, functools.partial(put_right, 1))
     sides = []
     for i, (who, slot) in enumerate(((after, 0), (before, 2))):
         copy = pltpu.make_async_remote_copy(
@@ -223,57 +285,33 @@
         copy.start()
         sides.append(copy)
 
-    loads["bases"].wait()
-    loads["upl"].wait()
-    cc = jnp.zeros((16, 64), F32)
-    for l in range(leaf_dev):
-        x16 = stack16(st[1, 16:24, l * 128 : (l + 1) * 128])
-        high, low = halves(bases_v[l])
-        bhi[l], blo[l] = high, low
-        two_high = jnp.concatenate([high, high], axis=0)
-        two_low = jnp.concatenate([low, low], axis=0)
-        c2 = fold(nt(x16, two_high) + nt(x16, two_low))
-        coef2[l] = c2
-        high, low = halves(upl_v[l])
-        uhi[l], ulo[l] = high, low
-        cc = cc + nn(stack16(c2), jnp.concatenate([high, low], axis=0))
-    cc = fold(cc)
-    loads["upc"].wait()
-    term = split_dot(nn, stack16(cc), upc_v[0])
-    ctz[z] = jnp.concatenate([cc, term], axis=1)
-    exchange(ctz, z, z_peer, side, 1)
-
-    arrived(reqz.at[pl.ds(0, side - 1)], x_recv.at[0])
-    row8 = iota((8, 128), 0)
-    tile = reqz[0]
-    for i in range(1, side):
-        tile = jnp.where(row8 == i, reqz[i], tile)
-    reqy[y] = tile
-    exchange(reqy, y, y_peer, side, 2)
-
-    def features(block, m):
-        a = st[block, 0:16, pl.ds(pl.multiple_of(m * 128, 128), 128)]
-        return a, 0.75 * jnp.sum(a * a, axis=0, keepdims=True)
-
-    def put_right(block, m):
-        b, norm = features(block, m)
-        high, mid, low = thirds(b)
-        parts = [high, mid, high, mid, low, high, norm_rows(norm, 0)]
-        right[block * leaf_dev + m] = jnp.concatenate(parts, axis=0).T.astype(BF16)
-        x = st[block, 16:24, pl.ds(pl.multiple_of(m * 128, 128), 128)]
-        top = rounded(x)
-        first = jnp.concatenate([top, x - top], axis=0)
-        second = jnp.concatenate([top, jnp.zeros_like(top)], axis=0)
-        weight[block * leaf_dev + m] = jnp.concatenate([first, second], axis=1).astype(BF16)
-
-    def put_left(l):
-        a, norm = features(1, l)
-        high, mid, low = thirds(-1.5 * a)
-        parts = [high, high, mid, mid, high, low, norm_rows(norm, 3)]
-        left[l] = jnp.concatenate(parts, axis=0).astype(BF16)
-
-    loop(0, leaf_dev, 4, put_left)
-    loop(0, leaf_dev, 4, functools.partial(put_right, 1))
+
+    loads["cpl"].wait()
+    loads["cpg"].wait()
+
+    def put_far(l):
+        parts = [cpl_v[l, k] for k in range(far_two)]
+        u = upl_v[l]
+        parts += [u, jnp.zeros_like(u)]
+        high, low = halves(jnp.concatenate(parts, axis=1))
+        turned = jnp.concatenate([high, low], axis=0).T
+        bh, bl = bhi[l], blo[l]
+        both = nn(turned, jnp.concatenate([bh, bh], axis=0))
+        both = both + nn(turned, jnp.concatenate([bl, bl], axis=0))
+        high, low = halves(both)
+        wide = far_two * 64
+        vhi[l], vlo[l] = high[:wide], low[:wide]
+        columns = pl.ds(pl.multiple_of(l * 128, 128), 128)
+        whi[:, columns], wlo[:, columns] = high[wide : wide + 64], low[wide : wide + 64]
+
+    loop(0, leaf_dev, 4, put_far)
+    uc_high, uc_low = halves(upc_v[0])
+    pieces = []
+    for h in range(n_grp):
+        high, low = halves(cpg_v[0, h])
+        other = jnp.where(grp == h, 0.0, 1.0).astype(F32)
+        pieces.append(other * (nn(uc_high, high) + nn(uc_high, low) + nn(uc_low, high)))
+    ghi[...], glo[...] = halves(jnp.concatenate(pieces, axis=1))
 
     arrived(ctz.at[pl.ds(0, side - 1)], x_recv.at[1])
     low_lanes = iota((8, 128), 1) < 64
@@ -285,10 +323,10 @@
     cty[y, side // 2] = total
     exchange(cty, y, y_peer, side, 3)
 
-    arrived(reqy.at[pl.ds(0, side - 1)], x_recv.at[2])
+    arrived(asked_by.at[pl.ds(0, n_leaf - 1)], x_recv.at[0])
     lane8 = iota((8, 128), 1)
-    for i in range(side):
-        asked = reqy[i]
+    for i in range(n_leaf // 8):
+        asked = asked_by[i * 8 : (i + 1) * 8]
         mine = (asked >> 4) == dev
         code = (lane8 * 16 + (asked & 15)).astype(F32)
         first = jnp.min(jnp.where(mine, code, 4096.0), axis=1, keepdims=True)
@@ -312,26 +350,30 @@
         ).start()
 
     loop(1, n_leaf, 7, send_row)
-
-    loads["cpl"].wait()
-
-    def put_coupling(l):
-        parts = [cpl_v[l, k] for k in range(far_two)]
-        high, low = halves(jnp.concatenate(parts, axis=1))
-        chi[l], clo[l] = high, low
-
-    loop(0, leaf_dev, 4, put_coupling)
-
     arrived(cty.at[pl.ds(0, side - 1)], x_recv.at[3])
     total = cty[0, side // 2]
     for i in range(1, side):
         total = total + cty[i, side // 2]
-    gcb[grp] = total
+    gcb[grp] = jnp.where(low_lanes, pltpu.roll(total, 64, 1), total)
     exchange(gcb, grp, g_peer, n_grp, 4)
+
+    loads["cpc"].wait()
+    loads["farc"].wait()
+    field_cluster = jnp.zeros((8, 64), F32)
+    for k in range(cpc_v.shape[1]):
+        f = jnp.clip(farc_s[0, k] - grp * n_leaf, 0, n_leaf - 1)
+        fy, fz = lax.div(f, side), lax.rem(f, side)
+        pair = cty[fy, lax.div(fz, 2)]
+        flag = jnp.full((8, 128), lax.rem(fz, 2), I32)
+        one = jnp.where(flag == 1, pltpu.roll(pair, 64, 1), pair)[:, :64]
+        field_cluster = field_cluster + split_dot(nt, stack16(one), cpc_v[0, k])
+    near_fc[...] = field_cluster
 
     for copy, block in zip(sides, (0, 2)):
         copy.wait_recv()
         loop(0, leaf_dev, 4, functools.partial(put_right, block))
+    loads["near"].wait()
+    loads["count"].wait()
     slots = near_s.shape[0]
     base = (dev - 1) * leaf_dev
 
@@ -354,24 +396,10 @@
     loop(0, leaf_dev, 4, near_leaf)
 
     arrived(gcb.at[pl.ds(0, n_grp - 1)], x_recv.at[4])
-    loads["cpc"].wait()
-    loads["cpg"].wait()
-    field_group = jnp.zeros((8, 64), F32)
-    for h in range(n_grp):
-        other = jnp.where(grp == h, 0.0, 1.0).astype(F32)
-        gc = gcb[h][:, 64:] * other
-        field_group = field_group + split_dot(nt, stack16(gc), cpg_v[0, h])
-    field_cluster = split_dot(nt, stack16(field_group), upc_v[0])
-    for k in range(cpc_v.shape[1]):
-        f = jnp.clip(farc_s[0, k] - grp * n_leaf, 0, n_leaf - 1)
-        fy, fz = lax.div(f, side), lax.rem(f, side)
-        pair = cty[fy, lax.div(fz, 2)]
-        flag = jnp.full((8, 128), lax.rem(fz, 2), I32)
-        one = jnp.where(flag == 1, pltpu.roll(pair, 64, 1), pair)[:, :64]
-        field_cluster = field_cluster + split_dot(nt, stack16(one), cpc_v[0, k])
-    fc16 = stack16(field_cluster)
-    for l in range(leaf_dev):
-        down[l] = fold(nt(fc16, uhi[l]) + nt(fc16, ulo[l]))
+    chunks = [jnp.where(low_lanes, gcb[2 * i], gcb[2 * i + 1]) for i in range(n_grp // 2)]
+    x16 = stack16(jnp.concatenate(chunks, axis=1))
+    fc16 = stack16(fold(nt(x16, ghi[...]) + nt(x16, glo[...])) + near_fc[...])
+    down[...] = fold(nn(fc16, whi[...]) + nn(fc16, wlo[...]))
 
     arrived(rows_in, x_recv.at[5])
     tab_copy.wait()
@@ -386,14 +414,15 @@
                 both.append(jnp.where(flag == half, got, pltpu.roll(got, 64, 1)))
             chunks.append(jnp.where(low_lanes, both[0], both[1]))
         x16 = stack16(jnp.concatenate(chunks, axis=1))
-        field = fold(nt(x16, chi[l]) + nt(x16, clo[l])) + down[l]
-        f16 = stack16(field)
-        out_ref[:, l * 128 : (l + 1) * 128] = fold(nn(f16, bhi[l]) + nn(f16, blo[l])) + near_out[l]
+        part = fold(nn(x16, vhi[l]) + nn(x16, vlo[l]))
+        columns = slice(l * 128, (l + 1) * 128)
+        out_ref[:, columns] = part + (down[:, columns] + near_out[l])
 
     for copy in sides:
         copy.wait_send()
-    for i, buf, n in ((0, reqz, side), (1, ctz, side), (2, reqy, side), (3, cty, side), (4, gcb, n_grp)):
+    for i, buf, n in ((1, ctz, side), (3, cty, side), (4, gcb, n_grp)):
         arrived(buf.at[pl.ds(0, n - 1)], x_send.at[i])
+    arrived(asked_by.at[pl.ds(0, n_leaf - 1)], x_send.at[0])
     arrived(rows_out, x_send.at[5])
 
 
@@ -417,14 +446,16 @@
     nrhs = rhs.shape[0]
     far_two = far_leaf.shape[1]
     anywhere = pl.BlockSpec(memory_space=pltpu.HBM)
-    scalars = pl.BlockSpec(memory_space=pltpu.SMEM)
     vmem = pltpu.VMEM
     return pl.pallas_call(
         functools.partial(kernel, side, n_grp),
         out_shape=vmem(rhs.shape, F32),
-        in_specs=[scalars] * 3 + [anywhere] * 9,
+        in_specs=[anywhere] * 12,
         out_specs=pl.BlockSpec(memory_space=vmem),
         scratch_shapes=[
+            pltpu.SMEM(near_list.shape[::-1], I32),
+            pltpu.SMEM(near_count.shape, I32),
+            pltpu.SMEM(far_cluster.shape, I32),
             vmem((3, 24, points.shape[1]), F32),
             vmem(bases.shape, F32),
             vmem(up_leaf.shape, F32),
@@ -435,27 +466,30 @@
             vmem(far_leaf.shape[::-1], I32),
             vmem(bases.shape, BF16),
             vmem(bases.shape, BF16),
-            vmem(up_leaf.shape, BF16),
-            vmem(up_leaf.shape, BF16),
-            vmem((leaf_dev, rank, far_two * rank), BF16),
-            vmem((leaf_dev, rank, far_two * rank), BF16),
+            vmem((leaf_dev, far_two * rank, width), BF16),
+            vmem((leaf_dev, far_two * rank, width), BF16),
+            vmem((rank, rhs.shape[1]), BF16),
+            vmem((rank, rhs.shape[1]), BF16),
+            vmem((rank, n_grp * rank), BF16),
+            vmem((rank, n_grp * rank), BF16),
             vmem((leaf_dev, width, 128), BF16),
             vmem((3 * leaf_dev, 128, width), BF16),
             vmem((3 * leaf_dev, 16, 2 * width), BF16),
             vmem((leaf_dev, nrhs, 128), F32),
             vmem((leaf_dev, nrhs, width), F32),
-            vmem((leaf_dev, nrhs, rank), F32),
+            vmem(rhs.shape, F32),
+            vmem((nrhs, rank), F32),
             vmem((1, 128), I32),
             pltpu.SMEM((1, 128), I32),
             vmem((n_leaf, 128), I32),
-            vmem((side, 8, 128), I32),
-            vmem((side, 8, 128), I32),
+            vmem((1, 128), I32),
+            vmem((n_leaf, 128), I32),
             vmem((side, 8, 128), F32),
             vmem((side, side // 2 + 1, 8, 128), F32),
             vmem((n_grp, 8, 128), F32),
             vmem((n_leaf - 1, 8, 128), F32),
             vmem((n_leaf - 1, 8, 128), F32),
-            pltpu.SemaphoreType.DMA((9,)),
+            pltpu.SemaphoreType.DMA((12,)),
             pltpu.SemaphoreType.DMA,
             pltpu.SemaphoreType.DMA((2,)),
             pltpu.SemaphoreType.DMA((2,)),

time: 42 us -> 36.2 us (0.86)
  Pallas kernels: 41.2 us -> 35.2 us
    pallas_call x1, Pallas kernels: 41.2 us -> 35.2 us  [per_device(): pl.pallas_call(functools.partial(kernel, side, n_grp), out_shape=vmem(rhs...]
where the time goes in v3:
time: 36.2 us; the launch traced here: 35.9 us
  Pallas kernels  35.2 us (97%)
  local copies, waits for them, and re-layouts  0.63 us (2%)
    pallas_call x1, Pallas kernels, per_device(): pl.pallas_call(functools.partial(kernel, side, n_grp), out_shape=vmem(rhs...  35.2 us

profile of v3, /device:TPU:1, one launch (start us, length us, event | category | flops | bytes accessed | tf_op | source)
XLA Modules:
  0.0 35.9 jit_solution(1301484290055172620)
XLA Ops:
  0.0 35.2 %shard_map.118 = f32[8,2048]{1,0:T(8,128)S(1)} custom-call(s32[8,16]{1,0:T(8,128)} %bitcast.2, s32[16]{0:T(128)} %count_h.1, s32[1,4]{1,0:T(1,128)} %farc_h.1, f32[16,2048]{1,0:T(8,128)} %pts_h.1, f32[8,2048]{1,0:T(8,128)} %rhs_h.1, f32[16,64,128]{2,1,0:T(8,128)} %bases_h.1, f32[16,64,64]{2,1,0:T(8,128)} %upl_h.1, f32[1,64,64]{2,1,0:T(8,128)} %upc_h.1, ...), custom_call_target="tpu_custom_call" | custom-call | tf_op jit(solution)/shard_map/pallas_call | solution.py:450
  35.3 0.6 %copy.14 = f32[8,2048]{1,0:T(8,128)} copy(f32[8,2048]{1,0:T(8,128)S(1)} %shard_map.118) | data formatting | bytes 131072

commit v4 on v3

--- a/solution.py
+++ b/solution.py
@@ -119,6 +119,7 @@
     asked_by,
     ctz,
     cty,
+    sums,
     gcb,
     rows_out,
     rows_in,
@@ -318,9 +319,10 @@
     total = ctz[0]
     for i in range(1, side):
         total = total + ctz[i]
+    sums[y] = total
+    exchange(sums, y, y_peer, side, 2)
     for i in range(side // 2):
         cty[y, i] = jnp.where(low_lanes, ctz[2 * i], pltpu.roll(ctz[2 * i + 1], 64, 1))
-    cty[y, side // 2] = total
     exchange(cty, y, y_peer, side, 3)
 
     arrived(asked_by.at[pl.ds(0, n_leaf - 1)], x_recv.at[0])
@@ -350,24 +352,12 @@
         ).start()
 
     loop(1, n_leaf, 7, send_row)
-    arrived(cty.at[pl.ds(0, side - 1)], x_recv.at[3])
-    total = cty[0, side // 2]
+    arrived(sums.at[pl.ds(0, side - 1)], x_recv.at[2])
+    total = sums[0]
     for i in range(1, side):
-        total = total + cty[i, side // 2]
+        total = total + sums[i]
     gcb[grp] = jnp.where(low_lanes, pltpu.roll(total, 64, 1), total)
     exchange(gcb, grp, g_peer, n_grp, 4)
-
-    loads["cpc"].wait()
-    loads["farc"].wait()
-    field_cluster = jnp.zeros((8, 64), F32)
-    for k in range(cpc_v.shape[1]):
-        f = jnp.clip(farc_s[0, k] - grp * n_leaf, 0, n_leaf - 1)
-        fy, fz = lax.div(f, side), lax.rem(f, side)
-        pair = cty[fy, lax.div(fz, 2)]
-        flag = jnp.full((8, 128), lax.rem(fz, 2), I32)
-        one = jnp.where(flag == 1, pltpu.roll(pair, 64, 1), pair)[:, :64]
-        field_cluster = field_cluster + split_dot(nt, stack16(one), cpc_v[0, k])
-    near_fc[...] = field_cluster
 
     for copy, block in zip(sides, (0, 2)):
         copy.wait_recv()
@@ -394,6 +384,19 @@
         near_out[l] = fold(acc)
 
     loop(0, leaf_dev, 4, near_leaf)
+
+    arrived(cty.at[pl.ds(0, side - 1)], x_recv.at[3])
+    loads["cpc"].wait()
+    loads["farc"].wait()
+    field_cluster = jnp.zeros((8, 64), F32)
+    for k in range(cpc_v.shape[1]):
+        f = jnp.clip(farc_s[0, k] - grp * n_leaf, 0, n_leaf - 1)
+        fy, fz = lax.div(f, side), lax.rem(f, side)
+        pair = cty[fy, lax.div(fz, 2)]
+        flag = jnp.full((8, 128), lax.rem(fz, 2), I32)
+        one = jnp.where(flag == 1, pltpu.roll(pair, 64, 1), pair)[:, :64]
+        field_cluster = field_cluster + split_dot(nt, stack16(one), cpc_v[0, k])
+    near_fc[...] = field_cluster
 
     arrived(gcb.at[pl.ds(0, n_grp - 1)], x_recv.at[4])
     chunks = [jnp.where(low_lanes, gcb[2 * i], gcb[2 * i + 1]) for i in range(n_grp // 2)]
@@ -420,7 +423,7 @@
 
     for copy in sides:
         copy.wait_send()
-    for i, buf, n in ((1, ctz, side), (3, cty, side), (4, gcb, n_grp)):
+    for i, buf, n in ((1, ctz, side), (2, sums, side), (3, cty, side), (4, gcb, n_grp)):
         arrived(buf.at[pl.ds(0, n - 1)], x_send.at[i])
     arrived(asked_by.at[pl.ds(0, n_leaf - 1)], x_send.at[0])
     arrived(rows_out, x_send.at[5])
@@ -485,7 +488,8 @@
             vmem((1, 128), I32),
             vmem((n_leaf, 128), I32),
             vmem((side, 8, 128), F32),
-            vmem((side, side // 2 + 1, 8, 128), F32),
+            vmem((side, side // 2, 8, 128), F32),
+            vmem((side, 8, 128), F32),
             vmem((n_grp, 8, 128), F32),
             vmem((n_leaf - 1, 8, 128), F32),
             vmem((n_leaf - 1, 8, 128), F32),

time: 36.2 us -> 34.9 us (0.964)
  the two profiles are of different devices: /device:TPU:1 before, /device:TPU:4 now
where the time goes in v4:
time: 34.9 us; the launch traced here: 34.8 us
  Pallas kernels  34.1 us (98%)
  local copies, waits for them, and re-layouts  0.63 us (2%)
    pallas_call x1, Pallas kernels, per_device(): pl.pallas_call(functools.partial(kernel, side, n_grp), out_shape=vmem(rhs...  34.1 us

profile of v4, /device:TPU:4, one launch (start us, length us, event | category | flops | bytes accessed | tf_op | source)
XLA Modules:
  0.0 34.8 jit_solution(4628100931078579177)
XLA Ops:
  0.0 34.1 %shard_map.118 = f32[8,2048]{1,0:T(8,128)S(1)} custom-call(s32[8,16]{1,0:T(8,128)} %bitcast.2, s32[16]{0:T(128)} %count_h.1, s32[1,4]{1,0:T(1,128)} %farc_h.1, f32[16,2048]{1,0:T(8,128)} %pts_h.1, f32[8,2048]{1,0:T(8,128)} %rhs_h.1, f32[16,64,128]{2,1,0:T(8,128)} %bases_h.1, f32[16,64,64]{2,1,0:T(8,128)} %upl_h.1, f32[1,64,64]{2,1,0:T(8,128)} %upc_h.1, ...), custom_call_target="tpu_custom_call" | custom-call | tf_op jit(solution)/shard_map/pallas_call | solution.py:453
  34.1 0.6 %copy.14 = f32[8,2048]{1,0:T(8,128)} copy(f32[8,2048]{1,0:T(8,128)S(1)} %shard_map.118) | data formatting | bytes 131072

commit v5 on v4

--- a/solution.py
+++ b/solution.py
@@ -142,17 +142,6 @@
 
     after, before = at_dev(lax.rem(dev + 1, many)), at_dev(lax.rem(dev + many - 1, many))
 
-    barrier = pltpu.get_barrier_semaphore()
-
-    def greet(who):
-        pl.semaphore_signal(barrier, inc=1, device_id=who, device_id_type=MESH)
-
-    greet(after)
-    greet(before)
-
-    loop(1, n_leaf, 7, lambda j: greet((grp, lax.rem(leaf + j, n_leaf))))
-    loop(1, n_grp, 7, lambda j: greet((lax.rem(grp + j, n_grp), leaf)))
-
     loads = {}
     plan = (
         ("farl", farl_h, farl_v),
@@ -170,7 +159,25 @@
     )
     for i, (name, src, dst) in enumerate(plan):
         loads[name] = pltpu.make_async_copy(src, dst, load_sem.at[i])
+    first = ("rhs", "bases", "upl", "farl", "upc")
+    for name in first:
         loads[name].start()
+
+
+    barrier = pltpu.get_barrier_semaphore()
+
+    def greet(who):
+        pl.semaphore_signal(barrier, inc=1, device_id=who, device_id_type=MESH)
+
+    greet(after)
+    greet(before)
+
+    loop(1, n_leaf, 7, lambda j: greet((grp, lax.rem(leaf + j, n_leaf))))
+    loop(1, n_grp, 7, lambda j: greet((lax.rem(grp + j, n_grp), leaf)))
+
+    for name, copy in loads.items():
+        if name not in first:
+            copy.start()
 
     def exchange(buf, at, peer, count, i):
         def go(j):

time: 34.9 us -> 34.5 us (0.989)
    pallas_call x1, Pallas kernels: 34.1 us -> 33.8 us  [per_device(): pl.pallas_call(functools.partial(kernel, side, n_grp), out_shape=vmem(rhs...]
where the time goes in v5:
time: 34.5 us; the launch traced here: 34.4 us
  Pallas kernels  33.8 us (98%)
  local copies, waits for them, and re-layouts  0.63 us (2%)
    pallas_call x1, Pallas kernels, per_device(): pl.pallas_call(functools.partial(kernel, side, n_grp), out_shape=vmem(rhs...  33.8 us

profile of v5, /device:TPU:4, one launch (start us, length us, event | category | flops | bytes accessed | tf_op | source)
XLA Modules:
  0.0 34.4 jit_solution(3191664423082067738)
XLA Ops:
  0.0 33.8 %shard_map.118 = f32[8,2048]{1,0:T(8,128)S(1)} custom-call(s32[8,16]{1,0:T(8,128)} %bitcast.2, s32[16]{0:T(128)} %count_h.1, s32[1,4]{1,0:T(1,128)} %farc_h.1, f32[16,2048]{1,0:T(8,128)} %pts_h.1, f32[8,2048]{1,0:T(8,128)} %rhs_h.1, f32[16,64,128]{2,1,0:T(8,128)} %bases_h.1, f32[16,64,64]{2,1,0:T(8,128)} %upl_h.1, f32[1,64,64]{2,1,0:T(8,128)} %upc_h.1, ...), custom_call_target="tpu_custom_call" | custom-call | tf_op jit(solution)/shard_map/pallas_call | solution.py:460
  33.8 0.6 %copy.14 = f32[8,2048]{1,0:T(8,128)} copy(f32[8,2048]{1,0:T(8,128)S(1)} %shard_map.118) | data formatting | bytes 131072

commit v6 on v5

--- a/solution.py
+++ b/solution.py
@@ -342,7 +342,8 @@
         last = jnp.max(jnp.where(mine, code, 0.0), axis=1, keepdims=True)
         ridx[i * 8 : (i + 1) * 8] = jnp.where(low_lanes, first, last).astype(I32) & 15
 
-    def send_row(j):
+    def send_row(i):
+        j = lax.rem(i * 27, n_leaf)
         who = lax.rem(leaf + j, n_leaf)
         index = jnp.broadcast_to(ridx[pl.ds(who, 1), :], (8, 128))
         picked = coef2[0]

time: 34.5 us -> 34.4 us (level)
  the two profiles are of different devices: /device:TPU:4 before, /device:TPU:2 now
where the time goes in v6:
time: 34.4 us; the launch traced here: 34.3 us
  Pallas kernels  33.6 us (98%)
  local copies, waits for them, and re-layouts  0.63 us (2%)
    pallas_call x1, Pallas kernels, per_device(): pl.pallas_call(functools.partial(kernel, side, n_grp), out_shape=vmem(rhs...  33.6 us

profile of v6, /device:TPU:2, one launch (start us, length us, event | category | flops | bytes accessed | tf_op | source)
XLA Modules:
  0.0 34.3 jit_solution(9517868906433073504)
XLA Ops:
  0.0 33.6 %shard_map.118 = f32[8,2048]{1,0:T(8,128)S(1)} custom-call(s32[8,16]{1,0:T(8,128)} %bitcast.2, s32[16]{0:T(128)} %count_h.1, s32[1,4]{1,0:T(1,128)} %farc_h.1, f32[16,2048]{1,0:T(8,128)} %pts_h.1, f32[8,2048]{1,0:T(8,128)} %rhs_h.1, f32[16,64,128]{2,1,0:T(8,128)} %bases_h.1, f32[16,64,64]{2,1,0:T(8,128)} %upl_h.1, f32[1,64,64]{2,1,0:T(8,128)} %upc_h.1, ...), custom_call_target="tpu_custom_call" | custom-call | tf_op jit(solution)/shard_map/pallas_call | solution.py:461
  33.6 0.6 %copy.14 = f32[8,2048]{1,0:T(8,128)} copy(f32[8,2048]{1,0:T(8,128)S(1)} %shard_map.118) | data formatting | bytes 131072

commit v7 on v6

--- a/solution.py
+++ b/solution.py
@@ -172,7 +172,7 @@
     greet(after)
     greet(before)
 
-    loop(1, n_leaf, 7, lambda j: greet((grp, lax.rem(leaf + j, n_leaf))))
+    loop(1, n_leaf, 7, lambda j: greet((grp, lax.rem(leaf + j * 27, n_leaf))))
     loop(1, n_grp, 7, lambda j: greet((lax.rem(grp + j, n_grp), leaf)))
 
     for name, copy in loads.items():
@@ -251,7 +251,7 @@
             dst_ref=asked_by.at[pl.ds(leaf, 1)],
             send_sem=x_send.at[0],
             recv_sem=x_recv.at[0],
-            device_id=(grp, lax.rem(leaf + j, n_leaf)),
+            device_id=(grp, lax.rem(leaf + j * 27, n_leaf)),
             device_id_type=MESH,
         ).start()
 

time: 34.4 us -> 34.9 us (1.015)
  the two profiles are of different devices: /device:TPU:2 before, /device:TPU:1 now
where the time goes in v7:
time: 34.9 us; the launch traced here: 34.2 us
  Pallas kernels  33.6 us (96%)
  local copies, waits for them, and re-layouts  0.63 us (2%)
    pallas_call x1, Pallas kernels, per_device(): pl.pallas_call(functools.partial(kernel, side, n_grp), out_shape=vmem(rhs...  33.6 us

profile of v7, /device:TPU:1, one launch (start us, length us, event | category | flops | bytes accessed | tf_op | source)
XLA Modules:
  0.0 34.2 jit_solution(9729592260568770925)
XLA Ops:
  0.0 33.6 %shard_map.118 = f32[8,2048]{1,0:T(8,128)S(1)} custom-call(s32[8,16]{1,0:T(8,128)} %bitcast.2, s32[16]{0:T(128)} %count_h.1, s32[1,4]{1,0:T(1,128)} %farc_h.1, f32[16,2048]{1,0:T(8,128)} %pts_h.1, f32[8,2048]{1,0:T(8,128)} %rhs_h.1, f32[16,64,128]{2,1,0:T(8,128)} %bases_h.1, f32[16,64,64]{2,1,0:T(8,128)} %upl_h.1, f32[1,64,64]{2,1,0:T(8,128)} %upc_h.1, ...), custom_call_target="tpu_custom_call" | custom-call | tf_op jit(solution)/shard_map/pallas_call | solution.py:461
  33.6 0.6 %copy.14 = f32[8,2048]{1,0:T(8,128)} copy(f32[8,2048]{1,0:T(8,128)S(1)} %shard_map.118) | data formatting | bytes 131072
